TPU v7x, 32 devices: a whole 2x2x4 slice. The times are simulated.
32 devices in a mesh: section: 2 (over y), fsdp: 4 (over z), dp: 4 (over x, core).
Axes of the slice: x: 2, y: 2, z: 4, core: 2. Of those that a mesh axis runs over, the one named last changes fastest.
Arguments:
- inputs: bfloat16 [2, 16, 256, 1024], P(None, ('fsdp', 'dp')), may hold values from -6 to 6
- cotangent: bfloat16 [2, 16, 256, 1024], P(None, ('fsdp', 'dp')), may hold values from -6 to 6
- segments: int32 [2, 16, 256], P(None, ('fsdp', 'dp')), may hold values from 0 to 3, never falling along the last dimension, each value on 1 to 128 neighbouring positions
- norm_gain: bfloat16 [2, 1024], P('section', 'fsdp'), may hold values from 0.5 to 1.5
- in_weight: bfloat16 [2, 1024, 4384], P('section', 'fsdp'), may hold values from -0.1875 to 0.1875
- conv_weight: bfloat16 [2, 4, 2304], P('section', None, 'fsdp'), may hold values from -3 to 3
- conv_bias: bfloat16 [2, 2304], P('section', 'fsdp'), may hold values from -3 to 3
- dt_bias: bfloat16 [2, 32], P('section', 'fsdp'), may hold values from -3 to 0.5
- decay_log: bfloat16 [2, 32], P('section', 'fsdp'), may hold values from -3 to 1.5
- skip_gain: bfloat16 [2, 32], P('section', 'fsdp'), may hold values from 0.5 to 1.5
- gate_gain: bfloat16 [2, 2048], P('section', 'fsdp'), may hold values from 0.5 to 1.5
- out_weight: bfloat16 [2, 2048, 1024], P('section', 'fsdp'), may hold values from -0.125 to 0.125
Outputs:
- output: bfloat16 [2, 16, 256, 1024], P('section', ('fsdp', 'dp'))
- input_grad: float32 [2, 16, 256, 1024], P('section', ('fsdp', 'dp'))
- norm_gain_grad: float32 [2, 1024], P('section', 'fsdp')
- in_weight_grad: float32 [2, 1024, 4384], P('section', 'fsdp')
- conv_weight_grad: float32 [2, 4, 2304], P('section', None, 'fsdp')
- conv_bias_grad: float32 [2, 2304], P('section', 'fsdp')
- dt_bias_grad: float32 [2, 32], P('section', 'fsdp')
- decay_log_grad: float32 [2, 32], P('section', 'fsdp')
- skip_gain_grad: float32 [2, 32], P('section', 'fsdp')
- gate_gain_grad: float32 [2, 2048], P('section', 'fsdp')
- out_weight_grad: float32 [2, 2048, 1024], P('section', 'fsdp')
Inputs may be any that keep to these rules, and one draw needn't show every extreme that they name: `segments`: in each sequence the document numbers never fall; a document has 1 to 128 positions and one of them has exactly 128.
All inputs are finite; a program needn't handle non-finite values.
Results may differ from a plain program's by a relative error of at most 0.02.
Values may be sent and summed in bfloat16 or wider, within the bound.
No kernel may reach another device: no remote copies, remote signals or barrier semaphores. Data moves between devices by JAX's collectives and lax.ppermute only.
A program may use at most 320 MiB of HBM per device.

v0:
```python
import jax
import jax.numpy as jnp
from jax import lax
from jax.sharding import PartitionSpec as P

STRETCH = 256


EPS = 1e-05
HIGH = lax.Precision.HIGHEST


def shifted_2(value, axis, steps):
    count = lax.axis_size(axis)
    initial, last = (max(0, -steps), min(count, count - steps))
    return lax.ppermute(value, axis, [(source, source + steps) for source in range(initial, last)])


def for_sending(value):

    def short(part):
        return part.astype(jnp.bfloat16) if part.dtype == jnp.float32 else part

    return jax.tree.map(short, value)


def partner(value, axis, distance):
    mask = 2**distance
    pairs = [(source, source ^ mask) for source in range(lax.axis_size(axis))]
    return lax.ppermute(value, axis, pairs)


def rms_norm(value, gain):
    return value * lax.rsqrt(jnp.mean(value * value, axis=-1, keepdims=True) + EPS) * gain


def stretch_step(state, pieces):
    decay_in, inputs_dt, keys_b, queries_c, seg_block, before = pieces
    width = decay_in.shape[0]
    cumul = jnp.cumsum(decay_in, axis=0)
    order = jnp.arange(width)
    within = (order[:, None] >= order[None, :]) & (seg_block[:, None] == seg_block[None, :])
    gaps = cumul.T[:, :, None] - cumul.T[:, None, :]
    decay = jnp.where(within[None], jnp.exp(jnp.where(within[None], gaps, 0.0)), 0.0)
    scores = jnp.dot(queries_c, keys_b.T, precision=HIGH)
    mixed = jnp.einsum("hij,jhp->ihp", decay * scores[None], inputs_dt, precision=HIGH)
    carried = (seg_block == before).astype(jnp.float32)
    from_state = jnp.einsum("in,hpn->ihp", queries_c, state, precision=HIGH)
    mixed = mixed + from_state * (jnp.exp(cumul) * carried[:, None])[:, :, None]
    final = seg_block[-1]
    tail = jnp.where((seg_block == final)[:, None], jnp.exp(cumul[-1][None, :] - cumul), 0.0)
    keep = jnp.exp(cumul[-1]) * (final == before).astype(jnp.float32)
    state = state * keep[:, None, None] + jnp.einsum(
        "jhp,jn->hpn", inputs_dt * tail[:, :, None], keys_b, precision=HIGH
    )
    return (state, mixed)


def mixer(proj, seg, conv_weight, conv_bias, dt_bias, decay_log, skip_gain, gate_gain):
    length = proj.shape[0]
    inner = gate_gain.shape[0]
    heads = dt_bias.shape[0]
    conv_width = conv_bias.shape[0]
    state_size = (conv_width - inner) // 2
    head_dim = inner // heads
    taps = conv_weight.shape[0]
    gate = proj[:, :inner]
    stream = proj[:, inner : inner + conv_width]
    dt_raw = proj[:, inner + conv_width :]
    total = conv_bias + stream * conv_weight[taps - 1]
    for lag in range(1, taps):
        shifted = jnp.pad(stream, ((lag, 0), (0, 0)))[:length]
        earlier = jnp.pad(seg, (lag, 0), constant_values=-1)[:length]
        total = (
            total + jnp.where((earlier == seg)[:, None], shifted, 0.0) * conv_weight[taps - 1 - lag]
        )
    conv_out = jax.nn.silu(total)
    values = conv_out[:, :inner].reshape(length, heads, head_dim)
    keys_b = conv_out[:, inner : inner + state_size]
    queries_c = conv_out[:, inner + state_size :]
    step = jax.nn.softplus(dt_raw + dt_bias)
    decay_in = -jnp.exp(decay_log) * step
    inputs_dt = values * step[:, :, None]
    blocks = length // STRETCH
    seg_blocks = seg.reshape(blocks, STRETCH)
    before = jnp.concatenate([jnp.full((1,), -1, jnp.int32), seg_blocks[:-1, -1]])
    start = jnp.zeros((heads, head_dim, state_size), jnp.float32)
    _, mixed = lax.scan(
        jax.checkpoint(stretch_step),
        start,
        (
            decay_in.reshape(blocks, STRETCH, heads),
            inputs_dt.reshape(blocks, STRETCH, heads, head_dim),
            keys_b.reshape(blocks, STRETCH, state_size),
            queries_c.reshape(blocks, STRETCH, state_size),
            seg_blocks,
            before,
        ),
    )
    mixed = mixed.reshape(length, heads, head_dim) + skip_gain[None, :, None] * values
    gated = mixed.reshape(length, inner) * jax.nn.silu(gate)
    return rms_norm(gated, gate_gain)


def run_mixer(proj, seg, conv_weight, conv_bias, dt_bias, decay_log, skip_gain, gate_gain):
    return jax.vmap(mixer, in_axes=(0, 0, None, None, None, None, None, None))(
        proj, seg, conv_weight, conv_bias, dt_bias, decay_log, skip_gain, gate_gain
    )


def contract(left, right, left_dim, right_dim):
    return lax.dot_general(
        left, right, (((left_dim,), (right_dim,)), ((), ())), preferred_element_type=jnp.float32
    )


def unpack(gathered):
    return tuple((piece[0] for piece in gathered))


def small_floats(weights):
    return tuple((piece.astype(jnp.float32) for piece in weights[2:8]))


def layer_forward(stream_in, seg, weights):
    batch, length, width = stream_in.shape
    flat = stream_in.reshape(batch * length, width)
    normed = rms_norm(flat, weights[0].astype(jnp.float32)).astype(jnp.bfloat16)
    proj = jnp.dot(normed, weights[1], preferred_element_type=jnp.float32)
    mixed = run_mixer(proj.reshape(batch, length, -1), seg, *small_floats(weights))
    out = jnp.dot(
        mixed.reshape(batch * length, -1).astype(jnp.bfloat16),
        weights[8],
        preferred_element_type=jnp.float32,
    )
    return stream_in + out.reshape(batch, length, width)


def layer_backward(stream_in, grad_out, seg, weights):
    batch, length, width = stream_in.shape
    rows = batch * length
    flat = stream_in.reshape(rows, width)
    normed, pull_norm = jax.vjp(rms_norm, flat, weights[0].astype(jnp.float32))
    normed_low = normed.astype(jnp.bfloat16)
    proj = jnp.dot(normed_low, weights[1], preferred_element_type=jnp.float32)

    def mixer_local(proj_in, taps_w, taps_b, step_bias, decay_rates, skip_terms, norm_gains):
        return run_mixer(
            proj_in, seg, taps_w, taps_b, step_bias, decay_rates, skip_terms, norm_gains
        )

    mixed, pull_mix = jax.vjp(mixer_local, proj.reshape(batch, length, -1), *small_floats(weights))
    mixed_low = mixed.reshape(rows, -1).astype(jnp.bfloat16)
    grad_low = grad_out.reshape(rows, width).astype(jnp.bfloat16)
    out_grad = contract(mixed_low, grad_low, 0, 0)
    grad_mixed = contract(grad_low, weights[8], 1, 1)
    pulled = pull_mix(grad_mixed.reshape(mixed.shape))
    grad_proj = pulled[0].reshape(rows, -1).astype(jnp.bfloat16)
    in_grad = contract(normed_low, grad_proj, 0, 0)
    grad_normed = contract(grad_proj, weights[1], 1, 1)
    grad_stream, gain_grad = pull_norm(grad_normed)
    grad_in = grad_out + grad_stream.reshape(batch, length, width)
    return (grad_in, (gain_grad, in_grad) + tuple(pulled[1:]) + (out_grad,))


def shards(
    inputs,
    cotangent,
    segments,
    norm_gain,
    in_weight,
    conv_weight,
    conv_bias,
    dt_bias,
    decay_log,
    skip_gain,
    gate_gain,
    out_weight,
):
    first = lax.axis_index("section") == 0
    micro = inputs.shape[0]
    weights = unpack(
        (
            lax.all_gather(norm_gain, "fsdp", axis=1, tiled=True),
            lax.all_gather(in_weight, "fsdp", axis=1, tiled=True),
            lax.all_gather(conv_weight, "fsdp", axis=2, tiled=True),
            lax.all_gather(conv_bias, "fsdp", axis=1, tiled=True),
            lax.all_gather(dt_bias, "fsdp", axis=1, tiled=True),
            lax.all_gather(decay_log, "fsdp", axis=1, tiled=True),
            lax.all_gather(skip_gain, "fsdp", axis=1, tiled=True),
            lax.all_gather(gate_gain, "fsdp", axis=1, tiled=True),
            lax.all_gather(out_weight, "fsdp", axis=1, tiled=True),
        )
    )
    blank = jnp.zeros(inputs.shape[1:], jnp.float32)
    totals = tuple((jnp.zeros(piece.shape, jnp.float32) for piece in weights))
    received = []
    returned = []
    results = []
    input_grads = []
    for tick in range(2 * micro + 2):
        if tick % 2 == 0:
            fwd_mb = tick // 2
            bwd_mb = tick // 2 - 1
            fwd_ok = fwd_mb < micro
            bwd_ok = 0 <= bwd_mb < micro
            kind_first = 1 if fwd_ok else 0
            kind_second = 2 if bwd_ok else 0
            fwd_src = inputs[min(fwd_mb, micro - 1)].astype(jnp.float32)
            safe = min(max(bwd_mb, 0), micro - 1)
            bwd_src = received[safe].astype(jnp.float32) if bwd_ok else blank
            bwd_grad = cotangent[safe].astype(jnp.float32)
        else:
            fwd_mb = (tick - 1) // 2
            bwd_mb = (tick - 3) // 2
            fwd_ok = fwd_mb < micro
            bwd_ok = 0 <= bwd_mb < micro
            kind_first = 2 if bwd_ok else 0
            kind_second = 1 if fwd_ok else 0
            fwd_src = received[fwd_mb].astype(jnp.float32) if fwd_ok else blank
            safe = min(max(bwd_mb, 0), micro - 1)
            bwd_src = inputs[safe].astype(jnp.float32)
            bwd_grad = returned[safe].astype(jnp.float32) if bwd_ok else blank
        fwd_seg = segments[min(fwd_mb, micro - 1)]
        bwd_seg = segments[min(max(bwd_mb, 0), micro - 1)]
        kind = jnp.where(first, kind_first, kind_second).astype(jnp.int32)
        held = totals

        def spare_work():
            return (blank, blank, held)

        def forward_work():
            return (layer_forward(fwd_src, fwd_seg, weights), blank, held)

        def backward_work():
            grad_in, grads = layer_backward(bwd_src, bwd_grad, bwd_seg, weights)
            return (blank, grad_in, tuple((a + b for a, b in zip(held, grads))))

        result, grad_in, totals = lax.switch(kind, [spare_work, forward_work, backward_work])
        if tick % 2 == 0:
            if fwd_ok:
                received.append(shifted_2(result.astype(jnp.bfloat16), "section", 1))
            if bwd_ok:
                returned.append(shifted_2(grad_in.astype(jnp.bfloat16), "section", -1))
        else:
            if fwd_ok:
                results.append(result)
            if bwd_ok:
                input_grads.append(grad_in)
    half = micro // 2
    forward_out = jnp.stack(results)
    backward_out = jnp.stack(input_grads)
    payload = jnp.where(first, backward_out[half:], forward_out[:half])
    arrived = partner(for_sending(payload), "section", 0).astype(payload.dtype)
    output = jnp.where(first, arrived, forward_out[half:]).astype(jnp.bfloat16)
    input_grad = jnp.where(first, backward_out[:half], arrived)
    totals = tuple((piece[None] for piece in totals))
    owned = (
        lax.psum_scatter(
            totals[0].astype(jnp.bfloat16), "fsdp", scatter_dimension=1, tiled=True
        ).astype(jnp.float32),
        lax.psum_scatter(
            totals[1].astype(jnp.bfloat16), "fsdp", scatter_dimension=1, tiled=True
        ).astype(jnp.float32),
        lax.psum_scatter(
            totals[2].astype(jnp.bfloat16), "fsdp", scatter_dimension=2, tiled=True
        ).astype(jnp.float32),
        lax.psum_scatter(
            totals[3].astype(jnp.bfloat16), "fsdp", scatter_dimension=1, tiled=True
        ).astype(jnp.float32),
        lax.psum_scatter(
            totals[4].astype(jnp.bfloat16), "fsdp", scatter_dimension=1, tiled=True
        ).astype(jnp.float32),
        lax.psum_scatter(
            totals[5].astype(jnp.bfloat16), "fsdp", scatter_dimension=1, tiled=True
        ).astype(jnp.float32),
        lax.psum_scatter(
            totals[6].astype(jnp.bfloat16), "fsdp", scatter_dimension=1, tiled=True
        ).astype(jnp.float32),
        lax.psum_scatter(
            totals[7].astype(jnp.bfloat16), "fsdp", scatter_dimension=1, tiled=True
        ).astype(jnp.float32),
        lax.psum_scatter(
            totals[8].astype(jnp.bfloat16), "fsdp", scatter_dimension=1, tiled=True
        ).astype(jnp.float32),
    )
    summed = (
        lax.psum(owned[0].astype(jnp.bfloat16), "dp").astype(jnp.float32),
        lax.psum(owned[1].astype(jnp.bfloat16), "dp").astype(jnp.float32),
        lax.psum(owned[2].astype(jnp.bfloat16), "dp").astype(jnp.float32),
        lax.psum(owned[3].astype(jnp.bfloat16), "dp").astype(jnp.float32),
        lax.psum(owned[4].astype(jnp.bfloat16), "dp").astype(jnp.float32),
        lax.psum(owned[5].astype(jnp.bfloat16), "dp").astype(jnp.float32),
        lax.psum(owned[6].astype(jnp.bfloat16), "dp").astype(jnp.float32),
        lax.psum(owned[7].astype(jnp.bfloat16), "dp").astype(jnp.float32),
        lax.psum(owned[8].astype(jnp.bfloat16), "dp").astype(jnp.float32),
    )
    return (output, input_grad) + tuple(summed)


def solution(mesh):
    placed = (
        P(None, ("fsdp", "dp"), None, None),
        P(None, ("fsdp", "dp"), None, None),
        P(None, ("fsdp", "dp"), None),
        P("section", "fsdp"),
        P("section", "fsdp", None),
        P("section", None, "fsdp"),
        P("section", "fsdp"),
        P("section", "fsdp"),
        P("section", "fsdp"),
        P("section", "fsdp"),
        P("section", "fsdp"),
        P("section", "fsdp", None),
    )
    return jax.shard_map(
        shards,
        mesh=mesh,
        in_specs=placed,
        out_specs=(
            P("section", ("fsdp", "dp"), None, None),
            P("section", ("fsdp", "dp"), None, None),
            P("section", "fsdp"),
            P("section", "fsdp", None),
            P("section", None, "fsdp"),
            P("section", "fsdp"),
            P("section", "fsdp"),
            P("section", "fsdp"),
            P("section", "fsdp"),
            P("section", "fsdp"),
            P("section", "fsdp", None),
        ),
        check_vma=False,
    )
```

profile of v0, /device:TPU:0, one launch (start us, length us, event | category | flops | bytes accessed | tf_op | source)
XLA Modules:
  0.0 1407.9 jit_solution(985623381214650457)
XLA Ops:
  14.4 43.6 %all_gather.30 = bf16[1,4,2304]{1,0,2:T(2,128)(2,1)S(1)} all-gather(bf16[1,4,576]{1,0,2:T(2,128)(2,1)S(1)} %copy.1220), channel_id=1, replica_groups=mesh['section'=2,'fsdp'=4,'dp'=4] {'fsdp'}, dimensions={2}, use_global_device_ids=true | all-gather | bytes 23040 | tf_op jit(solution)/shard_map/all_gather | solution.py:186
  59.3 12.6 all_gather.34
  71.9 13.3 all_gather.28
  108.8 163.9 %all-gather.3.cloned.1.call-done = bf16[1,1024,4384]{2,1,0:T(8,128)(2,1)} async-done(((bf16[1,256,4384]{2,1,0:T(8,128)(2,1)}), bf16[1,1024,4384]{2,1,0:T(8,128)(2,1)}) %all-gather.3.cloned.1.call-update) | async-done | bytes 8978448 | tf_op jit(solution)/shard_map/all_gather | solution.py:185
  272.6 68.6 %conditional.6 = (bf16[1,256,1024]{2,1,0:T(8,128)(2,1)}, f32[1024]{0:T(1024)}, f32[1024,4384]{0,1:T(8,128)}, f32[4,2304]{1,0:T(4,128)S(1)}, f32[2304]{0:T(1024)}...) conditional(s32[]{:T(128)} %clamp.23, () %tuple.228, ...), branch_computations={%region_0.1_spmd, %region_1.6_spmd, %region_6.35_spmd} | conditional | flops 18413684736 | bytes 339045568 | solution.py:239
  289.4 11.4 fusion
  342.6 11.9 collective-permute-done
  365.2 48.5 %conditional.8 = (bf16[1,256,1024]{2,1,0:T(8,128)(2,1)}, bf16[1,256,1024]{2,1,0:T(8,128)(2,1)}, f32[1024]{0:T(1024)}, f32[1024,4384]{0,1:T(8,128)}, f32[4,2304]{...) conditional(s32[]{:T(128)} %clamp.21, (f32[1024]{0:T(1024)}, ...), branch_computations={%region_69.71_spmd, %region_70.76_spmd, %region_75.106_spmd} | conditional | flops 18425264128 | bytes 358020576 | solution.py:239
  385.0 11.4 fusion.210
  415.0 175.2 %collective-permute-start.1 = (bf16[1,256,1024]{2,1,0:T(8,128)(2,1)}, bf16[1,256,1024]{2,1,0:T(8,128)(2,1)S(1)}, u32[]{:S(2)}, u32[]{:S(2)}) collective-permute-start(bf16[1,256,1024]{2,1,0:T(8,128)(2,1)} %get-tuple-element.1839), channel_id=1, source_target_pairs={{0,16},{1,17},{2,18},{3,19},{4,20},{5,21},{6,22},{7,23},{8,24},{9,... | collective-permute-start | bytes 1572872 | tf_op jit(solution)/shard_map/ppermute | solution.py:16
  590.2 9.8 collective-permute-done.2
  602.5 154.5 %conditional.9 = (f32[1024]{0:T(1024)}, f32[1024,4384]{0,1:T(8,128)}, f32[4,2304]{1,0:T(4,128)S(1)}, f32[2304]{0:T(1024)}, f32[32]{0:T(128)}, /*index=5*/f32[32]...) conditional(s32[]{:T(128)} %clamp.20, (f32[1024]{0:T(1024)}, ...), branch_computations={%region_105.107_spmd, %region_106.112_spmd, %region_111.142_spmd} | conditional | flops 18425004032 | bytes 364154272 | solution.py:239
  623.3 11.2 fusion.555
  664.3 14.4 %fusion.562 = (f32[32,256]{1,0:T(8,128)}, f32[32,256]{1,0:T(8,128)}, f32[256,256]{1,0:T(8,128)S(1)}) fusion(f32[256,256]{1,0:T(8,128)S(1)} %fusion.655, f32[32,256]{1,0:T(8,128)S(1)} %bitcast_add_fusion.44, pred[256,256]{1,0:T(8,128)(4,1)S(1)} %fusion.644, f32[1,256,32,64]{1,3,2,0:T(8,128)} %broadcast_multiply_fusion.6, f32[1,256,32,64]{1,3,2,0:T(8,128)} %bitcast.2119), kind=kOutput, calls=%fused_computation.954 | convolution fusion | flops 1633599488 | bytes 4882432 | tf_op jit(solution)/shard_map/cond/branch_2_fun/transpose(jvp(vmap()))/while/body/eval_jaxpr/checkpoint/hij,jhp->ihp/dot_general | solution.py:46
  683.7 11.6 multiply_reduce_fusion.41
  724.6 16.3 %convolution_add_fusion.7 = f32[1024,4384]{0,1:T(8,128)} fusion(f32[1024,4384]{0,1:T(8,128)} %get-tuple-element.1628, f32[1,256,1024]{2,1,0:T(8,128)S(1)} %get-tuple-element.1604, f32[1024]{0:T(1024)S(1)} %copy-done.209, f32[256]{0:T(256)S(1)} %copy-done.265, f32[1,256,2048]{1,2,0:T(8,128)} %get-tuple-element.2384, f32[1,256,2304]{1,2,0:T(8,128)} %copy-done.63, ...), kind=kOutput, calls=%fused_computation.939 | convolution fusion | flops 2307121152 | bytes 41456640 | tf_op jit(solution)/shard_map/cond/branch_2_fun/dot_general | solution.py:112
  758.0 11.4 conditional.10
  770.6 51.3 %collective-permute-done.3 = bf16[1,256,1024]{2,1,0:T(8,128)(2,1)S(1)} collective-permute-done((bf16[1,256,1024]{2,1,0:T(8,128)(2,1)}, bf16[1,256,1024]{2,1,0:T(8,128)(2,1)S(1)}, u32[]{:S(2)}, u32[]{:S(2)}) %collective-permute-start.3) | collective-permute-done | bytes 524320 | tf_op jit(solution)/shard_map/ppermute | solution.py:16
  822.0 173.2 %conditional.11 = (f32[1024]{0:T(1024)}, f32[1024,4384]{0,1:T(8,128)}, f32[4,2304]{1,0:T(4,128)S(1)}, f32[2304]{0:T(1024)}, f32[32]{0:T(128)}, /*index=5*/f32[32...) conditional(s32[]{:T(128)} %clamp.18, (f32[1024]{0:T(1024)}, ...), branch_computations={%region_173.175_spmd, %region_174.176_spmd, %region_175.206_spmd} | conditional | flops 18425266176 | bytes 368484864 | solution.py:239
  843.6 11.2 fusion.812
  893.3 13.8 fusion.819
  913.6 12.5 multiply_reduce_fusion.63
  962.9 16.3 %convolution_add_fusion.13 = f32[1024,4384]{0,1:T(8,128)} fusion(f32[1024,4384]{0,1:T(8,128)} %get-tuple-element.1730, f32[1,256,1024]{2,1,0:T(8,128)S(1)} %copy-done.1, f32[1024]{0:T(1024)S(1)} %copy-done.213, f32[256]{0:T(256)S(1)} %copy-done.297, f32[1,256,2048]{1,2,0:T(8,128)} %get-tuple-element.2426, f32[1,256,2304]{1,2,0:T(8,128)} %copy-done.64, ...), kind=kOutput, calls=%fused_computation.1370 | convolution fusion | flops 2307121152 | bytes 41456640 | tf_op jit(solution)/shard_map/cond/branch_2_fun/dot_general | solution.py:112
  1001.3 9.9 convert_bitcast_fusion
  1020.3 55.2 %reduce-scatter.20.cloned.1.call-done = bf16[1,512,1024]{2,1,0:T(8,128)(2,1)} async-done(((bf16[1,2048,1024]{2,1,0:T(8,128)(2,1)}), bf16[1,512,1024]{2,1,0:T(8,128)(2,1)}) %reduce-scatter.20.cloned.1.call-update) | async-done | bytes 1048592 | tf_op jit(solution)/shard_map/reduce_scatter | solution.py:283
  1075.4 156.7 %reduce-scatter.18.cloned.1.call-done = bf16[1,256,4384]{1,2,0:T(8,128)(2,1)} async-done(((bf16[1,1024,4384]{1,2,0:T(8,128)(2,1)}), bf16[1,256,4384]{1,2,0:T(8,128)(2,1)}) %reduce-scatter.18.cloned.1.call-update) | async-done | bytes 2244624 | tf_op jit(solution)/shard_map/reduce_scatter | solution.py:262
  1236.2 11.6 all-reduce.159
  1255.8 21.2 %reduce-scatter.28.cloned.1.call-done = bf16[512,1]{1,0:T(8,128)(2,1)} async-done(((bf16[2048,1]{1,0:T(8,128)(2,1)}), bf16[512,1]{1,0:T(8,128)(2,1)}) %reduce-scatter.28.cloned.1.call-update) | async-done | bytes 1040
  1278.0 22.1 %reduce-scatter.26.cloned.1.call-done = bf16[576,1]{1,0:T(8,128)(2,1)} async-done(((bf16[2304,1]{1,0:T(8,128)(2,1)}), bf16[576,1]{1,0:T(8,128)(2,1)}) %reduce-scatter.26.cloned.1.call-update) | async-done | bytes 1168
  1301.1 22.3 %reduce-scatter.24.cloned.1.call-done = bf16[576,4]{1,0:T(8,128)(2,1)} async-done(((bf16[2304,4]{1,0:T(8,128)(2,1)}), bf16[576,4]{1,0:T(8,128)(2,1)}) %reduce-scatter.24.cloned.1.call-update) | async-done | bytes 4624
  1324.6 10.7 all-reduce.157
  1342.4 53.0 %all-reduce.163.cloned.1.call-done = (bf16[1,256,4384]{1,2,0:T(8,128)(2,1)}, bf16[1,512,1024]{2,1,0:T(8,128)(2,1)}) async-done(((bf16[1,256,4384]{1,2,0:T(8,128)(2,1)}, bf16[1,512,1024]{2,1,0:T(8,128)(2,1)}), (bf16[1,256,4384]{1,2,0:T(8,128)(2,1)}, bf16[1,512,1024]{2,1,0:T(8,128)(2,1)})) %all-reduce.163.cloned.1.call-update) | async-done | bytes 3293200 | tf_op jit(solution)/shard_map/psum | solution.py:289
  (691 shorter events, 377.1 us)
Async XLA Ops:
  7.2 101.6 %all-gather.5.cloned.1.call-start = ((), (), s32[]{:S(2)}) async-start(), calls=%async_computation.7 | async-start | bytes 5242880 | tf_op jit(solution)/shard_map/all_gather | solution.py:192
  7.9 264.7 %all-gather.3.cloned.1.call-start = ((), (), s32[]{:S(2)}) async-start(), calls=%async_computation.6 | async-start | bytes 11468800 | tf_op jit(solution)/shard_map/all_gather | solution.py:185
  12.1 47.1 %copy-start.351 = (bf16[1,576]{1,0:T(2,128)(2,1)S(1)}, bf16[1,576]{1,0:T(2,128)(2,1)}, u32[]{:S(2)}) copy-start(bf16[1,576]{1,0:T(2,128)(2,1)} %param.37) | copy-start | bytes 3460
  12.1 47.1 %copy-start.352 = (bf16[1,512]{1,0:T(2,128)(2,1)S(1)}, bf16[1,512]{1,0:T(2,128)(2,1)}, u32[]{:S(2)}) copy-start(bf16[1,512]{1,0:T(2,128)(2,1)} %param.41) | copy-start | bytes 3076
  12.1 59.8 %copy-start.373 = (bf16[1,256]{1,0:T(2,128)(2,1)S(1)}, bf16[1,256]{1,0:T(2,128)(2,1)}, u32[]{:S(2)}) copy-start(bf16[1,256]{1,0:T(2,128)(2,1)} %param.34) | copy-start | bytes 1540
  12.1 73.1 %copy-start.376 = (bf16[1,8]{1,0:T(2,128)(2,1)S(1)}, bf16[1,8]{1,0:T(2,128)(2,1)}, u32[]{:S(2)}) copy-start(bf16[1,8]{1,0:T(2,128)(2,1)} %param.38) | copy-start | bytes 52
  12.1 73.4 %copy-start.377 = (bf16[1,8]{1,0:T(2,128)(2,1)S(1)}, bf16[1,8]{1,0:T(2,128)(2,1)}, u32[]{:S(2)}) copy-start(bf16[1,8]{1,0:T(2,128)(2,1)} %param.39) | copy-start | bytes 52
  12.2 73.6 %copy-start.378 = (bf16[1,8]{1,0:T(2,128)(2,1)S(1)}, bf16[1,8]{1,0:T(2,128)(2,1)}, u32[]{:S(2)}) copy-start(bf16[1,8]{1,0:T(2,128)(2,1)} %param.40) | copy-start | bytes 52
  12.2 83.7 %copy-start.353 = (s32[2,1,256]{2,1,0:T(1,128)S(1)}, s32[2,1,256]{2,1,0:T(1,128)}, u32[]{:S(2)}) copy-start(s32[2,1,256]{2,1,0:T(1,128)} %param.33) | copy-start | bytes 6148
  12.2 84.3 %copy-start.92 = (bf16[2,1,256,1024]{3,2,1,0:T(8,128)(2,1)S(1)}, bf16[2,1,256,1024]{3,2,1,0:T(8,128)(2,1)}, u32[]{:S(2)}) copy-start(bf16[2,1,256,1024]{3,2,1,0:T(8,128)(2,1)} %param.32) | copy-start | bytes 3145732
  12.2 1063.2 %reduce-scatter.20.cloned.1.call-start = ((), (), s32[]{:S(2)}) async-start(), calls=%async_computation.9 | async-start | bytes 5242880 | tf_op jit(solution)/shard_map/reduce_scatter | solution.py:283
  95.9 176.7 %copy-start.244 = (bf16[32]{0:T(256)(128)(2,1)}, bf16[32]{0:T(256)(128)(2,1)S(1)}, u32[]{:S(2)}) copy-start(bf16[32]{0:T(256)(128)(2,1)S(1)} %get-tuple-element.2239) | copy-start | bytes 196
  96.5 176.1 %copy-start.200 = (s32[1,256]{1,0:T(1,128)}, s32[1,256]{1,0:T(1,128)S(1)}, u32[]{:S(2)}) copy-start(s32[1,256]{1,0:T(1,128)S(1)} %get-tuple-element.2450) | copy-start | bytes 3076
  341.2 13.3 collective-permute-start
  413.7 188.8 %copy-start.201 = (s32[1,256]{1,0:T(1,128)S(1)}, s32[1,256]{1,0:T(1,128)}, u32[]{:S(2)}) copy-start(s32[1,256]{1,0:T(1,128)} %copy-done.200) | copy-start | bytes 3076
  413.7 188.8 %copy-start.224 = (s32[1,256]{1,0:T(1,128)S(1)}, s32[1,256]{1,0:T(1,128)}, u32[]{:S(2)}) copy-start(s32[1,256]{1,0:T(1,128)} %get-tuple-element.2451) | copy-start | bytes 3076
  413.7 186.3 %collective-permute-start.2 = (bf16[1,256,1024]{2,1,0:T(8,128)(2,1)}, bf16[1,256,1024]{2,1,0:T(8,128)(2,1)S(1)}, u32[]{:S(2)}, u32[]{:S(2)}) collective-permute-start(bf16[1,256,1024]{2,1,0:T(8,128)(2,1)} %get-tuple-element.1840), channel_id=1, source_target_pairs={{16,0},{17,1},{18,2},{19,3},{20,4},{21,5},{22,6},{23,7},{24,8},{25... | collective-permute-start | bytes 1572872 | tf_op jit(solution)/shard_map/ppermute | solution.py:16
  415.0 186.3 %collective-permute-start.1 = (bf16[1,256,1024]{2,1,0:T(8,128)(2,1)}, bf16[1,256,1024]{2,1,0:T(8,128)(2,1)S(1)}, u32[]{:S(2)}, u32[]{:S(2)}) collective-permute-start(bf16[1,256,1024]{2,1,0:T(8,128)(2,1)} %get-tuple-element.1839), channel_id=1, source_target_pairs={{0,16},{1,17},{2,18},{3,19},{4,20},{5,21},{6,22},{7,23},{8,24},{9,... | collective-permute-start | bytes 1572872 | tf_op jit(solution)/shard_map/ppermute | solution.py:16
  769.3 52.6 %collective-permute-start.3 = (bf16[1,256,1024]{2,1,0:T(8,128)(2,1)}, bf16[1,256,1024]{2,1,0:T(8,128)(2,1)S(1)}, u32[]{:S(2)}, u32[]{:S(2)}) collective-permute-start(bf16[1,256,1024]{2,1,0:T(8,128)(2,1)} %get-tuple-element.1859), channel_id=1, source_target_pairs={{16,0},{17,1},{18,2},{19,3},{20,4},{21,5},{22,6},{23,7},{24,8},{25... | collective-permute-start | bytes 1572872 | tf_op jit(solution)/shard_map/ppermute | solution.py:16
  822.1 39.0 %copy-start.61 = (f32[1,256,1024]{2,1,0:T(8,128)}, f32[1,256,1024]{2,1,0:T(8,128)S(1)}, u32[]{:S(2)}) copy-start(f32[1,256,1024]{2,1,0:T(8,128)S(1)} %get-tuple-element.1716) | copy-start | bytes 3145732 | tf_op jit(solution)/shard_map/cond
  841.9 27.0 %copy-start.147 = (f32[256,32]{0,1:T(8,128)}, f32[256,32]{0,1:T(8,128)S(1)}, u32[]{:S(2)}) copy-start(f32[256,32]{0,1:T(8,128)S(1)} %get-tuple-element.2428) | copy-start | bytes 98308 | tf_op jit(solution)/shard_map/cond
  893.3 20.3 %copy-start.239 = (bf16[32]{0:T(256)(128)(2,1)S(1)}, bf16[32]{0:T(256)(128)(2,1)}, u32[]{:S(2)}) copy-start(bf16[32]{0:T(256)(128)(2,1)} %get-tuple-element.1719) | copy-start | bytes 196 | tf_op jit(solution)/shard_map/cond
  913.6 23.9 %copy-start.119 = (f32[256,32]{1,0:T(8,128)S(1)}, f32[256,32]{1,0:T(8,128)}, u32[]{:S(2)}) copy-start(f32[256,32]{1,0:T(8,128)} %get-tuple-element.2309) | copy-start | bytes 98308 | tf_op jit(solution)/shard_map/cond
  1001.3 230.8 %reduce-scatter.18.cloned.1.call-start = ((), (), s32[]{:S(2)}) async-start(), calls=%async_computation.8 | async-start | bytes 11223040 | tf_op jit(solution)/shard_map/reduce_scatter | solution.py:262
  1011.2 243.7 %reduce-scatter.22.cloned.1.call-start = ((), (), s32[]{:S(2)}) async-start(), calls=%async_computation.10 | async-start | bytes 327680
  1013.6 263.4 %reduce-scatter.28.cloned.1.call-start = ((), (), s32[]{:S(2)}) async-start(), calls=%async_computation.13 | async-start | bytes 655360
  1015.5 284.6 %reduce-scatter.26.cloned.1.call-start = ((), (), s32[]{:S(2)}) async-start(), calls=%async_computation.12 | async-start | bytes 737280
  1016.8 306.6 %reduce-scatter.24.cloned.1.call-start = ((), (), s32[]{:S(2)}) async-start(), calls=%async_computation.11 | async-start | bytes 737280
  1019.5 212.6 %copy-start.96 = (bf16[1,1,256,1024]{3,2,1,0:T(8,128)(2,1)S(1)}, bf16[1,1,256,1024]{3,2,1,0:T(8,128)(2,1)}, u32[]{:S(2)}) copy-start(bf16[1,1,256,1024]{3,2,1,0:T(8,128)(2,1)} %get-tuple-element.1860) | copy-start | bytes 1572868
  1019.5 375.9 %all-reduce.163.cloned.1.call-start = ((), (), s32[]{:S(2)}) async-start(), calls=%async_computation.14 | async-start | bytes 6586368 | tf_op jit(solution)/shard_map/psum | solution.py:289
  1232.1 107.0 %copy-start.91 = (f32[1,1,256,1024]{3,2,1,0:T(8,128)S(1)}, f32[1,1,256,1024]{3,2,1,0:T(8,128)}, u32[]{:S(2)}) copy-start(f32[1,1,256,1024]{3,2,1,0:T(8,128)} %copy-done.90) | copy-start | bytes 3145732
  1232.2 106.9 %collective-permute-start.4 = (bf16[1,1,256,1024]{3,2,1,0:T(8,128)(2,1)S(1)}, bf16[1,1,256,1024]{3,2,1,0:T(8,128)(2,1)S(1)}, u32[]{:S(2)}, u32[]{:S(2)}) collective-permute-start(bf16[1,1,256,1024]{3,2,1,0:T(8,128)(2,1)S(1)} %select_convert_fusion), channel_id=1, source_target_pairs={{0,16},{16,0},{1,17},{17,1},{2,18},{18,2},{3,19},{19,3},{4,20},{20... | collective-permute-start | bytes 1572872 | tf_op jit(solution)/shard_map/ppermute | solution.py:30
  (142 other events, 876.7 us)
Sparse Core Ops, SparseCore 0:
  9.6 99.1 all-gather.4
  110.9 161.6 all-gather.2
  1001.4 73.9 reduce-scatter.19
  1077.8 154.2 reduce-scatter.17
  1234.3 20.5 reduce-scatter.21
  1257.0 19.9 reduce-scatter.27
  1279.8 20.2 reduce-scatter.25
  1303.0 20.3 reduce-scatter.23
  1325.9 69.5 all-reduce.162
where the time goes:
time: 1420 us; the launch traced here: 1410 us
  waiting for transfers between devices  584 us (41%)
  matrix products  242 us (17%)
  starting transfers between devices  182 us (13%)
  other arithmetic  150 us (11%)
  blocking collectives  101 us (7%)
  local copies, waits for them, and re-layouts  81.7 us (6%)
  loops' own time  49.9 us (4%)
  between operations  16.5 us (1%)
    ppermute x4, starting transfers between devices, shifted_2(): lax.ppermute(value, axis, [(source, source + steps) for source in range(i...  179 us
    all_gather x1, waiting for transfers between devices, shards(): lax.all_gather(in_weight, 'fsdp', axis=1, tiled=True)  164 us
    reduce_scatter x1, waiting for transfers between devices, shards(): lax.psum_scatter(totals[1].astype(jnp.bfloat16), 'fsdp', scatter_dimensio...  157 us
    dot_general x8, matrix products, stretch_step(): jnp.einsum('hij,jhp->ihp', decay * scores[None], inputs_dt, precision=HIGH)  97.4 us
    unnamed x13, waiting for transfers between devices  73.3 us
    ppermute x4, waiting for transfers between devices, shifted_2(): lax.ppermute(value, axis, [(source, source + steps) for source in range(i...  73.2 us
    dot_general x8, matrix products, contract(): lax.dot_general(left, right, (((left_dim,), (right_dim,)), ((), ())), pre...  67.4 us
    reduce_scatter x1, waiting for transfers between devices, shards(): lax.psum_scatter(totals[8].astype(jnp.bfloat16), 'fsdp', scatter_dimensio...  55.2 us
  transfers between devices with their start and end apart: 14, of which 13 were waited for; matrix products, arithmetic and copies ran while one was open for 3% of the time, Pallas kernels for 0%

commit v1 on v0

v1 whole, which is shorter than its diff:
```python
import functools

import jax
import jax.numpy as jnp
from jax import lax
from jax.experimental import pallas as pl
from jax.experimental.pallas import tpu as pltpu
from jax.sharding import PartitionSpec as P

EPS = 1e-05
LOG2E = 1.4426950408889634
HIGH = lax.Precision.HIGHEST
F32 = jnp.float32
BF16 = jnp.bfloat16
LANES = 128
WIDE = 256
VMEM_BYTES = 56 * 1024 * 1024


def sigmoid(v):
    return 0.5 * jnp.tanh(0.5 * v) + 0.5


def dot(a, b):
    return lax.dot_general(a, b, (((1,), (0,)), ((), ())), preferred_element_type=F32)


def dot_nt(a, b):
    return lax.dot_general(a, b, (((1,), (1,)), ((), ())), preferred_element_type=F32)


def dot_tn(a, b):
    return lax.dot_general(a, b, (((0,), (0,)), ((), ())), preferred_element_type=F32)


def twice(v):
    return jnp.concatenate([v, v], axis=1)


def fold(v):
    return v[:, :LANES] + v[:, LANES:]


def cols(start, width=WIDE):
    return pl.ds(pl.multiple_of(start, LANES), width)


def write_masks(segc_ref, mask_ref, taps):
    seg = segc_ref[...]
    row = lax.broadcasted_iota(jnp.int32, seg.shape, 0)
    for lag in range(1, taps):
        same = (pltpu.roll(seg, lag, 0) == seg) & (row >= lag)
        mask_ref[lag - 1] = jnp.where(same, 1.0, 0.0)


def conv_chunk(s, start, cw_ref, cb_ref, mask_ref, taps):
    at = cols(start)
    total = cb_ref[:, at] + s * cw_ref[pl.ds(taps - 1, 1), at]
    for lag in range(1, taps):
        shifted = pltpu.roll(s, lag, 0) * twice(mask_ref[lag - 1])
        total = total + shifted * cw_ref[pl.ds(taps - 1 - lag, 1), at]
    return total


def step_sizes(dt, dtb_ref, dl_ref, heads):
    length = dt.shape[0]
    pad = jnp.zeros((length, LANES - heads), F32)
    v = jnp.concatenate([dt, pad], axis=1) + dtb_ref[...]
    step = jnp.maximum(v, 0.0) + jnp.log1p(jnp.exp(-jnp.abs(v)))
    rate = -jnp.exp(dl_ref[...]) * step
    i = lax.broadcasted_iota(jnp.int32, (length, length), 0)
    j = lax.broadcasted_iota(jnp.int32, (length, length), 1)
    lower = jnp.where(i >= j, 1.0, 0.0)
    scaled = rate * LOG2E
    cumul = lax.dot_general(lower, scaled, (((1,), (0,)), ((), ())), precision=HIGH, preferred_element_type=F32)
    return v, step, rate, cumul


def head_lanes(v, quad, per):
    return pltpu.roll(v, lax.rem(LANES - per * quad, LANES), 1)


def spread(v, i0, head_dim):
    length = v.shape[0]
    lane = lax.broadcasted_iota(jnp.int32, (length, LANES), 1)
    a = jnp.broadcast_to(v[:, i0 : i0 + 1], (length, LANES))
    b = jnp.broadcast_to(v[:, i0 + 1 : i0 + 2], (length, LANES))
    return jnp.where(lane < head_dim, a, b)


def forward_body(
    sizes, u_ref, segc_ref, segr_ref, ng_ref, cw_ref, cb_ref, dtb_ref, dl_ref, sk_ref, gg_ref, w_hbm, ow_hbm,
    out_ref, gate_ref, stream_ref, dt_ref, y_ref, normed_ref, mixed_ref,
    w, ow, mask_ref, s_ref, gated_ref, cum_ref, step_ref, cumt_ref, sem, osem,
):
    length, width, inner, conv, heads, taps = sizes
    state = (conv - inner) // 2
    head_dim = inner // heads
    per = WIDE // head_dim
    quads = inner // WIDE
    half = length // 2
    proj = w.shape[1]
    tail = 2 * inner

    def stream_copy(q):
        at = cols(inner + q * WIDE)
        return pltpu.make_async_copy(w_hbm.at[:, at], w.at[:, at], sem.at[1 + 2 * q])

    def gate_copy(q):
        at = cols(q * WIDE)
        return pltpu.make_async_copy(w_hbm.at[:, at], w.at[:, at], sem.at[2 + 2 * q])

    tail_copy = pltpu.make_async_copy(
        w_hbm.at[:, tail:proj], w.at[:, tail:proj], sem.at[0]
    )
    tail_copy.start()
    for q in range(quads):
        stream_copy(q).start()
        gate_copy(q).start()
    out_copy = pltpu.make_async_copy(ow_hbm, ow, osem)
    out_copy.start()

    u = u_ref[...].astype(F32)
    scale = lax.rsqrt(jnp.mean(u * u, axis=-1, keepdims=True) + EPS)
    normed_ref[...] = (u * scale * ng_ref[...]).astype(BF16)
    write_masks(segc_ref, mask_ref, taps)

    tail_copy.wait()
    dt = dot(normed_ref[...], w[:, inner + conv : proj])
    dt_ref[...] = dt
    _, step, _, cumul = step_sizes(dt, dtb_ref, dl_ref, heads)
    step_ref[...] = step
    cum_ref[...] = cumul
    cumt_ref[...] = jnp.transpose(cumul)

    def conv_of(start, s):
        low = s.astype(BF16)
        stream_ref[:, cols(start)] = low
        total = conv_chunk(low.astype(F32), start, cw_ref, cb_ref, mask_ref, taps)
        return total * sigmoid(total)

    bc = conv_of(inner, dot(normed_ref[...], w[:, tail : tail + 2 * state]))
    keys = bc[:, :state].astype(BF16)
    queries = bc[:, state:].astype(BF16)
    i = lax.broadcasted_iota(jnp.int32, (length, length), 0)
    j = lax.broadcasted_iota(jnp.int32, (length, length), 1)
    within = (i >= j) & (segc_ref[:, :1] == segr_ref[:1, :])
    s_ref[...] = jnp.where(within, dot_nt(queries, keys), 0.0)

    def quad_step(q, squares):
        at = cols(q * WIDE)
        stream_copy(q).wait()
        gate_copy(q).wait()
        x = conv_of(q * WIDE, dot(normed_ref[...], w[:, cols(inner + q * WIDE)]))
        z = dot(normed_ref[...], w[:, at]).astype(BF16)
        gate_ref[:, at] = z
        z = z.astype(F32)
        cum_q = head_lanes(cum_ref[...], q, per)
        step_q = head_lanes(step_ref[...], q, per)
        ys = []
        for pair in range(per // 2):
            part = slice(pair * LANES, (pair + 1) * LANES)
            xdt = (x[:, part] * spread(step_q, 2 * pair, head_dim)).astype(BF16)
            got = []
            for k in range(2):
                h = 2 * pair + k
                col = cum_q[:, h : h + 1]
                row = cumt_ref[pl.ds(per * q + h, 1), :]
                top = jnp.exp2(jnp.minimum(col[:half] - row[:, :half], 0.0)) * s_ref[:half, :half]
                low = jnp.exp2(jnp.minimum(col[half:] - row, 0.0)) * s_ref[half:, :]
                got.append(
                    jnp.concatenate(
                        [dot(top.astype(BF16), xdt[:half]), dot(low.astype(BF16), xdt)], axis=0
                    )
                )
            lane = lax.broadcasted_iota(jnp.int32, (length, LANES), 1)
            ys.append(jnp.where(lane < head_dim, got[0], got[1]))
        y = jnp.concatenate(ys, axis=1)
        y_ref[:, at] = y
        gated = (y + sk_ref[:, at] * x) * (z * sigmoid(z))
        gated_ref[:, at] = gated
        return squares + fold(gated * gated)

    squares = lax.fori_loop(0, quads, quad_step, jnp.zeros((length, LANES), F32))
    scale2 = lax.rsqrt(jnp.sum(squares, axis=-1, keepdims=True) * (1.0 / inner) + EPS)

    def mixed_step(q, _):
        at = cols(q * WIDE)
        mixed_ref[:, at] = (gated_ref[:, at] * scale2 * gg_ref[:, at]).astype(BF16)
        return 0

    lax.fori_loop(0, quads, mixed_step, 0)
    out_copy.wait()

    def out_step(n, _):
        at = cols(n * WIDE)
        out_ref[:, at] = (u_ref[:, at].astype(F32) + dot(mixed_ref[...], ow[:, at])).astype(BF16)
        return 0

    lax.fori_loop(0, width // WIDE, out_step, 0)


def vmem():
    return pl.BlockSpec(memory_space=pltpu.VMEM)


def hbm():
    return pl.BlockSpec(memory_space=pl.ANY)


def forward(u, seg_col, seg_row, small, w, ow):
    length, width = u.shape
    ng, cw, cb, dtb, dl, sk, gg, heads = small
    inner, conv, taps = gg.shape[1], cb.shape[1], cw.shape[0]
    proj = w.shape[1]
    quads = inner // WIDE
    shape = jax.ShapeDtypeStruct
    return pl.pallas_call(
        functools.partial(forward_body, (length, width, inner, conv, heads, taps)),
        out_shape=(
            shape((length, width), BF16),
            shape((length, inner), BF16),
            shape((length, conv), BF16),
            shape((length, heads), F32),
            shape((length, inner), F32),
            shape((length, width), BF16),
            shape((length, inner), BF16),
        ),
        in_specs=[vmem()] * 10 + [hbm()] * 2,
        out_specs=[vmem()] * 7,
        scratch_shapes=[
            pltpu.VMEM((width, proj), BF16),
            pltpu.VMEM((inner, width), BF16),
            pltpu.VMEM((taps - 1, length, LANES), F32),
            pltpu.VMEM((length, length), F32),
            pltpu.VMEM((length, inner), F32),
            pltpu.VMEM((length, LANES), F32),
            pltpu.VMEM((length, LANES), F32),
            pltpu.VMEM((LANES, length), F32),
            pltpu.SemaphoreType.DMA((1 + 2 * quads,)),
            pltpu.SemaphoreType.DMA,
        ],
        compiler_params=pltpu.CompilerParams(vmem_limit_bytes=VMEM_BYTES),
        cost_estimate=pl.CostEstimate(
            flops=2 * length * (width * proj + inner * width + 2 * length * inner),
            bytes_accessed=2 * (width * proj + inner * width),
            transcendentals=length * (length * heads + 2 * inner),
        ),
        name="layer_forward",
    )(u, seg_col, seg_row, ng, cw, cb, dtb, dl, sk, gg, w, ow)


def backward_body(
    sizes, u_ref, g_ref, segc_ref, segr_ref, ng_ref, cw_ref, cb_ref, dtb_ref, dl_ref, sk_ref, gg_ref,
    gate_ref, stream_ref, dt_ref, y_ref, w_hbm, ow_hbm,
    dlow_ref, gin_ref, dng_ref, dcw_ref, dcb_ref, ddtb_ref, ddl_ref, dsk_ref, dgg_ref,
    w, ow, mask_ref, x_ref, slope_ref, dm_ref, st_ref, dst_ref, cum_ref, step_ref, cumt_ref, heads_ref, direct_ref,
    dn_ref, sem, osem,
):
    length, width, inner, conv, heads, taps = sizes
    state = (conv - inner) // 2
    head_dim = inner // heads
    per = WIDE // head_dim
    quads = inner // WIDE
    half = length // 2
    proj = w.shape[1]

    def out_copy(q):
        at = pl.ds(pl.multiple_of(q * WIDE, WIDE), WIDE)
        return pltpu.make_async_copy(ow_hbm.at[at, :], ow.at[at, :], osem.at[q])

    for q in range(quads):
        out_copy(q).start()
    in_copy = pltpu.make_async_copy(w_hbm, w, sem)
    in_copy.start()

    write_masks(segc_ref, mask_ref, taps)
    v, step, rate, cumul = step_sizes(dt_ref[...], dtb_ref, dl_ref, heads)
    step_ref[...] = step
    cum_ref[...] = cumul
    cumt_ref[...] = jnp.transpose(cumul)
    heads_ref[...] = jnp.zeros_like(heads_ref)
    direct_ref[...] = jnp.zeros_like(direct_ref)
    dst_ref[...] = jnp.zeros_like(dst_ref)

    def conv_of(start):
        at = cols(start)
        total = conv_chunk(stream_ref[:, at].astype(F32), start, cw_ref, cb_ref, mask_ref, taps)
        sig = sigmoid(total)
        x = total * sig
        x_ref[:, at] = x
        slope_ref[:, at] = sig + x * (1.0 - sig)
        return x

    def first_step(q, carry):
        squares, cross = carry
        at = cols(q * WIDE)
        out_copy(q).wait()
        dm = dot_nt(g_ref[...], ow[pl.ds(pl.multiple_of(q * WIDE, WIDE), WIDE), :])
        x = conv_of(q * WIDE)
        z = gate_ref[:, at].astype(F32)
        gated = (y_ref[:, at] + sk_ref[:, at] * x) * (z * sigmoid(z))
        dm_ref[:, at] = dm
        return squares + fold(gated * gated), cross + fold(gated * (dm * gg_ref[:, at]))

    zero = jnp.zeros((length, LANES), F32)
    squares, cross = lax.fori_loop(0, quads, first_step, (zero, zero))
    scale2 = lax.rsqrt(jnp.sum(squares, axis=-1, keepdims=True) * (1.0 / inner) + EPS)
    back2 = jnp.sum(cross, axis=-1, keepdims=True) * scale2 * scale2 * scale2 * (1.0 / inner)

    bc = conv_of(inner)
    keys = bc[:, :state].astype(BF16)
    queries = bc[:, state:].astype(BF16)
    j = lax.broadcasted_iota(jnp.int32, (length, length), 0)
    i = lax.broadcasted_iota(jnp.int32, (length, length), 1)
    within = (i >= j) & (segc_ref[:, :1] == segr_ref[:1, :])
    st_ref[...] = jnp.where(within, dot_nt(keys, queries), 0.0)

    def conv_back(start, d_conv):
        at = cols(start)
        d_total = d_conv * slope_ref[:, at]
        s = stream_ref[:, at].astype(F32)
        dcb_ref[:, at] = jnp.sum(d_total, axis=0, keepdims=True)
        dcw_ref[pl.ds(taps - 1, 1), at] = jnp.sum(d_total * s, axis=0, keepdims=True)
        d_stream = d_total * cw_ref[pl.ds(taps - 1, 1), at]
        for lag in range(1, taps):
            back = pltpu.roll(d_total * twice(mask_ref[lag - 1]), length - lag, 0)
            dcw_ref[pl.ds(taps - 1 - lag, 1), at] = jnp.sum(back * s, axis=0, keepdims=True)
            d_stream = d_stream + back * cw_ref[pl.ds(taps - 1 - lag, 1), at]
        dlow_ref[:, cols(inner + start)] = d_stream.astype(BF16)

    def second_step(q, _):
        at = cols(q * WIDE)
        x = x_ref[:, at]
        y = y_ref[:, at]
        dm = dm_ref[:, at]
        z = gate_ref[:, at].astype(F32)
        sig = sigmoid(z)
        zs = z * sig
        yf = y + sk_ref[:, at] * x
        gated = yf * zs
        scaled = dm * scale2
        dgg_ref[:, at] = jnp.sum(scaled * gated, axis=0, keepdims=True)
        d_gated = scaled * gg_ref[:, at] - gated * back2
        dy = d_gated * zs
        dlow_ref[:, at] = (d_gated * yf * (sig + zs * (1.0 - sig))).astype(BF16)
        dsk_ref[:, at] = jnp.sum(dy * x, axis=0, keepdims=True)
        dy_low = dy.astype(BF16)
        cum_q = head_lanes(cum_ref[...], q, per)
        step_q = head_lanes(step_ref[...], q, per)
        lane = lax.broadcasted_iota(jnp.int32, (length, LANES), 1)
        dst_top = jnp.zeros((half, length), F32)
        dst_low = jnp.zeros((half, half), F32)
        xdts, dxdts, steps = [], [], []
        for pair in range(per // 2):
            part = slice(pair * LANES, (pair + 1) * LANES)
            step_p = spread(step_q, 2 * pair, head_dim)
            xdt = (x[:, part] * step_p).astype(BF16)
            dyp = dy_low[:, part]
            got = []
            for k in range(2):
                h = 2 * pair + k
                mine = (lane < head_dim) if k == 0 else (lane >= head_dim)
                xm = jnp.where(mine, xdt.astype(F32), 0.0).astype(BF16)
                col = cum_q[:, h : h + 1]
                row = cumt_ref[pl.ds(per * q + h, 1), :]
                decay_top = jnp.exp2(jnp.minimum(row - col[:half], 0.0))
                decay_low = jnp.exp2(jnp.minimum(row[:, half:] - col[half:], 0.0))
                top = (decay_top * st_ref[:half, :]).astype(BF16)
                low = (decay_low * st_ref[half:, half:]).astype(BF16)
                got.append(jnp.concatenate([dot(top, dyp), dot(low, dyp[half:])], axis=0))
                dst_top = dst_top + dot_nt(xm[:half], dyp) * decay_top
                dst_low = dst_low + dot_nt(xm[half:], dyp[half:]) * decay_low
            xdts.append(xdt.astype(F32))
            steps.append(step_p)
            dxdts.append(jnp.where(lane < head_dim, got[0], got[1]))
        dst_ref[:half, :] += dst_top
        dst_ref[half:, half:] += dst_low
        xdt = jnp.concatenate(xdts, axis=1)
        dxdt = jnp.concatenate(dxdts, axis=1)
        steps = jnp.concatenate(steps, axis=1)
        pick_row = lax.broadcasted_iota(jnp.int32, (WIDE, LANES), 0)
        pick_col = lax.broadcasted_iota(jnp.int32, (WIDE, LANES), 1)
        pick = jnp.where(pick_row // head_dim + per * q == pick_col, 1.0, 0.0).astype(BF16)
        both = dy_low.astype(F32) * y - xdt * dxdt
        high = both.astype(BF16)
        rest = (both - high.astype(F32)).astype(BF16)
        heads_ref[...] += dot(high, pick) + dot(rest, pick)
        direct_ref[...] += dot((dxdt * x).astype(BF16), pick)
        conv_back(q * WIDE, dxdt * steps + sk_ref[:, at] * dy)
        return 0

    lax.fori_loop(0, quads, second_step, 0)

    d_scores = jnp.where(within, dst_ref[...], 0.0).astype(BF16)
    conv_back(inner, jnp.concatenate([dot(d_scores, queries), dot_tn(d_scores, keys)], axis=1))

    upper = jnp.where(i >= j, 1.0, 0.0)
    d_rate = lax.dot_general(
        upper, heads_ref[...], (((1,), (0,)), ((), ())), precision=HIGH, preferred_element_type=F32
    )
    ddl_ref[...] = jnp.sum(d_rate * rate, axis=0, keepdims=True)
    d_step = direct_ref[...] - d_rate * jnp.exp(dl_ref[...])
    d_dt = d_step / (1.0 + jnp.exp(-v))
    ddtb_ref[...] = jnp.sum(d_dt, axis=0, keepdims=True)
    d_dt_low = d_dt[:, :heads].astype(BF16)
    dlow_ref[:, inner + conv : proj] = d_dt_low

    in_copy.wait()
    u = u_ref[...].astype(F32)
    scale = lax.rsqrt(jnp.mean(u * u, axis=-1, keepdims=True) + EPS)

    def normed_step(n, _):
        rows = pl.ds(pl.multiple_of(n * WIDE, WIDE), WIDE)
        dn_ref[:, cols(n * WIDE)] = dot_nt(dlow_ref[:, : inner + conv], w[rows, : inner + conv]) + dot_nt(
            d_dt_low, w[rows, inner + conv : proj]
        )
        return 0

    lax.fori_loop(0, width // WIDE, normed_step, 0)
    dn = dn_ref[...]
    dng_ref[...] = jnp.sum(dn * u * scale, axis=0, keepdims=True)
    dn = dn * ng_ref[...]
    back = jnp.mean(dn * u, axis=-1, keepdims=True) * scale * scale * scale
    gin_ref[...] = g_ref[...].astype(F32) + dn * scale - u * back


def backward(u, g, seg_col, seg_row, small, kept, w, ow):
    length, width = u.shape
    ng, cw, cb, dtb, dl, sk, gg, heads = small
    inner, conv, taps = gg.shape[1], cb.shape[1], cw.shape[0]
    proj = w.shape[1]
    quads = inner // WIDE
    gate, stream, dt, y = kept
    shape = jax.ShapeDtypeStruct
    return pl.pallas_call(
        functools.partial(backward_body, (length, width, inner, conv, heads, taps)),
        out_shape=(
            shape((length, proj), BF16),
            shape((length, width), F32),
            shape((1, width), F32),
            shape((taps, conv), F32),
            shape((1, conv), F32),
            shape((1, LANES), F32),
            shape((1, LANES), F32),
            shape((1, inner), F32),
            shape((1, inner), F32),
        ),
        in_specs=[vmem()] * 15 + [hbm()] * 2,
        out_specs=[vmem()] * 9,
        scratch_shapes=[
            pltpu.VMEM((width, proj), BF16),
            pltpu.VMEM((inner, width), BF16),
            pltpu.VMEM((taps - 1, length, LANES), F32),
            pltpu.VMEM((length, conv), F32),
            pltpu.VMEM((length, conv), F32),
            pltpu.VMEM((length, inner), F32),
            pltpu.VMEM((length, length), F32),
            pltpu.VMEM((length, length), F32),
            pltpu.VMEM((length, LANES), F32),
            pltpu.VMEM((length, LANES), F32),
            pltpu.VMEM((LANES, length), F32),
            pltpu.VMEM((length, LANES), F32),
            pltpu.VMEM((length, LANES), F32),
            pltpu.VMEM((length, width), F32),
            pltpu.SemaphoreType.DMA,
            pltpu.SemaphoreType.DMA((quads,)),
        ],
        compiler_params=pltpu.CompilerParams(vmem_limit_bytes=VMEM_BYTES),
        cost_estimate=pl.CostEstimate(
            flops=2 * length * (width * proj + inner * width + 4 * length * inner),
            bytes_accessed=2 * (width * proj + inner * width) + 8 * length * proj,
            transcendentals=length * (length * heads + 4 * inner),
        ),
        name="layer_backward",
    )(u, g, seg_col, seg_row, ng, cw, cb, dtb, dl, sk, gg, gate, stream, dt, y, w, ow)


def flip(value, axis, distance):
    pairs = [(source, source ^ distance) for source in range(lax.axis_size(axis))]
    return lax.ppermute(value, axis, pairs)


def rotate(value, axis):
    count = lax.axis_size(axis)
    return lax.ppermute(value, axis, [(source, (source + 1) % count) for source in range(count)])


def distances(axis):
    found, d = [], 1
    while d < lax.axis_size(axis):
        found.append(d)
        d *= 2
    return found


def after(value, *others):
    return lax.optimization_barrier((value,) + others)[0]


def gather_rows(shard, start=None):
    ring, share = lax.axis_size("fsdp"), lax.axis_size("dp")
    z, q = lax.axis_index("fsdp"), lax.axis_index("dp")
    rows, columns = shard.shape[0] // share, shard.shape[1]
    own = shard.reshape(share, rows, columns)
    whole = jnp.broadcast_to(own[None], (ring, share, rows, columns))
    travelling = lax.dynamic_index_in_dim(own, q, 0, keepdims=False)
    if start is not None:
        travelling = after(travelling, start)
    for step in range(1, ring):
        travelling = rotate(travelling, "fsdp")
        source = lax.rem(z - step + ring, ring)
        parts = {0: travelling}
        for d in reversed(distances("dp")):
            parts.update({m | d: flip(v, "dp", d) for m, v in list(parts.items())})
        for m, v in parts.items():
            whole = lax.dynamic_update_slice(whole, v[None, None], (source, q ^ m, 0, 0))
    return whole, travelling


def reduce_rows(left, right):
    ring, share, rows, depth = left.shape
    z, q = lax.axis_index("fsdp"), lax.axis_index("dp")
    columns = right.shape[1]
    order = [lax.rem(z + 2 * ring - 1 - s, ring) for s in range(ring)]
    steps = distances("dp")

    def block(mask):
        mine = lax.dynamic_index_in_dim(left, q ^ mask, 1, keepdims=False)
        mine = jnp.concatenate([lax.dynamic_index_in_dim(mine, at, 0) for at in order], axis=0)
        product = jnp.dot(mine.reshape(ring * rows, depth), right, preferred_element_type=jnp.float32)
        return product.astype(BF16).reshape(ring, rows, columns)

    def total(level, mask):
        if level == 0:
            return block(mask)
        d = steps[level - 1]
        away = total(level - 1, mask | d)
        if level == len(steps):
            arrived = [flip(away[s], "dp", d) for s in range(ring)]
            here = total(level - 1, mask)
            return [here[s].astype(F32) + arrived[s].astype(F32) for s in range(ring)]
        arrived = flip(away, "dp", d)
        here = total(level - 1, mask)
        return (here.astype(F32) + arrived.astype(F32)).astype(BF16)

    parts = total(len(steps), 0)
    value = parts[0]
    for s in range(1, ring):
        value = rotate(value.astype(BF16), "fsdp").astype(F32) + parts[s]
    value = value.astype(BF16)
    owned = {0: value}
    for d in reversed(steps):
        owned.update({m | d: flip(v, "dp", d) for m, v in list(owned.items())})
    whole = jnp.zeros((share, rows, columns), F32)
    for m, v in owned.items():
        whole = lax.dynamic_update_slice(whole, v.astype(F32)[None], (q ^ m, 0, 0))
    return whole.reshape(1, share * rows, columns)


def shards(
    inputs,
    cotangent,
    segments,
    norm_gain,
    in_weight,
    conv_weight,
    conv_bias,
    dt_bias,
    decay_log,
    skip_gain,
    gate_gain,
    out_weight,
):
    first = lax.axis_index("section") == 0
    z = lax.axis_index("fsdp")
    ring, share = lax.axis_size("fsdp"), lax.axis_size("dp")
    length, width = inputs.shape[2], inputs.shape[3]
    taps = conv_weight.shape[1]
    heads = dt_bias.shape[1] * ring
    inner = gate_gain.shape[1] * ring
    head_dim = inner // heads

    pieces = (norm_gain[0], conv_bias[0], dt_bias[0], decay_log[0], skip_gain[0], gate_gain[0], conv_weight[0].reshape(-1))
    sizes = [piece.shape[0] for piece in pieces]
    packed = lax.all_gather(jnp.concatenate(pieces), "fsdp", axis=0).astype(F32)
    fields, start = [], 0
    for size in sizes:
        fields.append(packed[:, start : start + size])
        start += size
    taps_w = fields[6].reshape(ring, taps, -1).transpose(1, 0, 2).reshape(taps, -1)
    rows = [field.reshape(1, -1) for field in fields[:6]]

    def lanes(row):
        return jnp.pad(row, ((0, 0), (0, LANES - heads)))

    small = (
        rows[0],
        taps_w,
        rows[1],
        lanes(rows[2]),
        lanes(rows[3]),
        jnp.repeat(rows[4], head_dim, axis=1),
        rows[5],
        heads,
    )
    w, last = gather_rows(in_weight[0])
    w = w.reshape(width, -1)
    ow, _ = gather_rows(out_weight[0], last)
    ow = ow.reshape(inner, width)

    seg = segments[:, 0].astype(F32)
    seg_cols = [jnp.broadcast_to(seg[m][:, None], (length, LANES)) for m in range(2)]
    seg_rows = [jnp.broadcast_to(seg[m][None], (8, length)) for m in range(2)]
    pick = functools.partial(jnp.where, first)

    def to_second(value):
        return lax.ppermute(value, "section", [(0, 1)])

    def to_first(value):
        return lax.ppermute(value, "section", [(1, 0)])

    u_a, u_b = inputs[0, 0], inputs[1, 0]
    g_a, g_b = cotangent[0, 0], cotangent[1, 0]

    out0 = forward(u_a, seg_cols[0], seg_rows[0], small, w, ow)[0]
    u1 = pick(u_b, to_second(out0))
    seg1 = pick(seg_cols[1], seg_cols[0]), pick(seg_rows[1], seg_rows[0])
    out1, gate1, stream1, dt1, y1, normed1, mixed1 = forward(u1, *seg1, small, w, ow)
    stream_b = to_second(out1)
    kept1 = (gate1, stream1, dt1, y1)
    back2 = backward(u1, g_a, *seg1, small, kept1, w, ow)
    grad_a = to_first(back2[1].astype(BF16))
    u3 = pick(u_a, stream_b)
    seg3 = pick(seg_cols[0], seg_cols[1]), pick(seg_rows[0], seg_rows[1])
    out3, gate3, stream3, dt3, y3, normed3, mixed3 = forward(u3, *seg3, small, w, ow)
    g4 = pick(grad_a, g_b)
    back4 = backward(u3, g4, *seg3, small, (gate3, stream3, dt3, y3), w, ow)
    grad_b = to_first(back4[1].astype(BF16))
    back5 = backward(u1, grad_b, *seg1, small, kept1, w, ow)

    output = pick(to_first(out1), out3)
    input_grad = pick(back4[1], to_second(back5[1].astype(BF16)).astype(F32))

    def by_owner(value):
        depth, count = value.shape
        return value.T.reshape(ring, share, count // ring // share, depth)

    mixed_t = by_owner(jnp.concatenate([mixed3, mixed1], axis=0))
    normed_t = by_owner(jnp.concatenate([normed3, normed1], axis=0))
    out_grad = reduce_rows(mixed_t, jnp.concatenate([g4, pick(grad_b, g_a)], axis=0))
    in_grad = reduce_rows(normed_t, jnp.concatenate([back4[0], pick(back5[0], back2[0])], axis=0))

    def added(k):
        return back4[k] + pick(back5[k], back2[k])

    grads = (
        added(2),
        added(4),
        added(5)[:, :heads],
        added(6)[:, :heads],
        jnp.sum(added(7).reshape(heads, head_dim), axis=1)[None],
        added(8),
    )
    taps_grad = added(3).reshape(taps, ring, -1).transpose(1, 0, 2).reshape(ring, -1)
    packed = jnp.concatenate([grad.reshape(ring, -1) for grad in grads] + [taps_grad], axis=1)
    packed = lax.psum(packed, ("fsdp", "dp"))
    packed = lax.dynamic_index_in_dim(packed, z, 0)
    fields, start = [], 0
    for size in sizes:
        fields.append(packed[:, start : start + size])
        start += size
    return (
        output[None, None],
        input_grad[None, None],
        fields[0],
        in_grad,
        fields[6].reshape(1, taps, -1),
        fields[1],
        fields[2],
        fields[3],
        fields[4],
        fields[5],
        out_grad,
    )


def solution(mesh):
    spread_over = ("fsdp", "dp")
    row = P("section", "fsdp")
    matrix = P("section", "fsdp", None)
    tap = P("section", None, "fsdp")
    activation = P(None, spread_over, None, None)
    result = P("section", spread_over, None, None)
    return jax.shard_map(
        shards,
        mesh=mesh,
        in_specs=(activation, activation, P(None, spread_over, None), row, matrix, tap, row, row, row, row, row, matrix),
        out_specs=(result, result, row, matrix, tap, row, row, row, row, row, matrix),
        check_vma=False,
    )
```

time: 1420 us -> 546 us (0.38)
  waiting for transfers between devices: 584 us -> 132 us
  matrix products: 242 us -> 24.7 us
  starting transfers between devices: 182 us -> 43.3 us
  Pallas kernels: 0 us -> 124 us
  other arithmetic: 150 us -> 45.9 us
  loops' own time: 49.9 us -> 0 us
    dot_general x44 -> x8, matrix products: 242 us -> 24.7 us  [block(): jnp.dot(mine.reshape(ring * rows, depth), right, preferred_element_type=j...]
    reduce_scatter x2 -> x0, waiting for transfers between devices: 212 us -> none  [the longest x1 157 us: shards(): lax.psum_scatter(totals[1].astype(jnp.bfloat16), 'fsdp', scatter_dimensio...]
    all_gather x2 -> x0, waiting for transfers between devices: 173 us -> none  [the longest x1 164 us: shards(): lax.all_gather(in_weight, 'fsdp', axis=1, tiled=True)]
    ppermute x5 -> x54, starting transfers between devices: 182 us -> 43.3 us  [the longest x36 23.8 us: flip(): return lax.ppermute(value, axis, pairs)]
    pallas_call x0 -> x6, Pallas kernels: none -> 124 us  [the longest x3 75.4 us: backward(): pl.pallas_call(functools.partial(backward_body, (length, width, inner, co...]
    unnamed x13 -> x0, waiting for transfers between devices: 73.3 us -> none
    all_gather x3 -> x0, blocking collectives: 69.5 us -> none  [the longest x1 43.6 us: shards(): lax.all_gather(conv_weight, 'fsdp', axis=2, tiled=True)]
    ppermute x5 -> x54, waiting for transfers between devices: 73.2 us -> 132 us  [the longest x36 59.1 us: flip(): return lax.ppermute(value, axis, pairs)]
  transfers between devices with their start and end apart: 14 -> 54, of which waited for: 13 -> 18; matrix products, arithmetic and copies ran while one was open for 3% -> 24% of each run, Pallas kernels for 0% -> 12%
where the time goes in v1:
time: 546 us; the launch traced here: 537 us
  waiting for transfers between devices  132 us (24%)
  Pallas kernels  124 us (23%)
  blocking collectives  88.8 us (16%)
  local copies, waits for them, and re-layouts  75.9 us (14%)
  other arithmetic  45.9 us (8%)
  starting transfers between devices  43.3 us (8%)
  matrix products  24.7 us (5%)
    pallas_call x3, Pallas kernels, backward(): pl.pallas_call(functools.partial(backward_body, (length, width, inner, co...  75.4 us
    psum x1, blocking collectives, shards(): packed = lax.psum(packed, ('fsdp', 'dp'))  64.5 us
    ppermute x36, waiting for transfers between devices, flip(): return lax.ppermute(value, axis, pairs)  59.1 us
    ppermute x12, waiting for transfers between devices, rotate(): lax.ppermute(value, axis, [(source, (source + 1) % count) for source in r...  58.1 us
    pallas_call x3, Pallas kernels, forward(): pl.pallas_call(functools.partial(forward_body, (length, width, inner, con...  48.2 us
    dot_general x8, matrix products, block(): jnp.dot(mine.reshape(ring * rows, depth), right, preferred_element_type=j...  24.7 us
    unnamed x1, blocking collectives  24.2 us
    ppermute x36, starting transfers between devices, flip(): return lax.ppermute(value, axis, pairs)  23.8 us
  transfers between devices with their start and end apart: 54, of which 18 were waited for; matrix products, arithmetic and copies ran while one was open for 24% of the time, Pallas kernels for 12%

profile of v1, /device:TPU:0, one launch (start us, length us, event | category | flops | bytes accessed | tf_op | source)
XLA Modules:
  0.0 536.7 jit_solution(9945759204798603880)
XLA Ops:
  9.5 24.2 %all-reduce.2 = bf16[14688]{0:T(1024)(128)(2,1)S(1)} all-reduce(bf16[14688]{0:T(1024)(128)(2,1)S(1)} %dynamic-update-slice), channel_id=2, replica_groups=mesh['section'=2,'fsdp'=4,'dp'=4] {'fsdp'}, use_global_device_ids=true, to_apply=%add.2 | all-reduce | flops 14688 | bytes 58752
  42.3 4.5 broadcast_in_dim.185
  48.8 10.9 %collective-permute-done.4 = bf16[64,4384]{1,0:T(8,128)(2,1)S(1)} collective-permute-done((bf16[64,4384]{1,0:T(8,128)(2,1)}, bf16[64,4384]{1,0:T(8,128)(2,1)S(1)}, u32[]{:S(2)}, u32[]{:S(2)}) %collective-permute-start.4) | collective-permute-done | bytes 561184 | tf_op jit(solution)/shard_map/ppermute | solution.py:486
  62.5 14.9 %collective-permute-done.8 = bf16[64,4384]{1,0:T(8,128)(2,1)S(1)} collective-permute-done((bf16[64,4384]{1,0:T(8,128)(2,1)S(1)}, bf16[64,4384]{1,0:T(8,128)(2,1)S(1)}, u32[]{:S(2)}, u32[]{:S(2)}) %collective-permute-start.8) | collective-permute-done | bytes 561184 | tf_op jit(solution)/shard_map/ppermute | solution.py:486
  81.5 5.7 %collective-permute-done.12 = bf16[128,1024]{1,0:T(8,128)(2,1)S(1)} collective-permute-done((bf16[128,1024]{1,0:T(8,128)(2,1)S(1)}, bf16[128,1024]{1,0:T(8,128)(2,1)S(1)}, u32[]{:S(2)}, u32[]{:S(2)}) %collective-permute-start.12) | collective-permute-done | bytes 262176 | tf_op jit(solution)/shard_map/ppermute | solution.py:486
  90.1 7.5 %collective-permute-done.13 = bf16[128,1024]{1,0:T(8,128)(2,1)S(1)} collective-permute-done((bf16[128,1024]{1,0:T(8,128)(2,1)S(1)}, bf16[128,1024]{1,0:T(8,128)(2,1)S(1)}, u32[]{:S(2)}, u32[]{:S(2)}) %collective-permute-start.13) | collective-permute-done | bytes 262176 | tf_op jit(solution)/shard_map/ppermute | solution.py:481
  104.6 8.3 %collective-permute-done.20 = bf16[128,1024]{1,0:T(8,128)(2,1)S(1)} collective-permute-done((bf16[128,1024]{1,0:T(8,128)(2,1)S(1)}, bf16[128,1024]{1,0:T(8,128)(2,1)S(1)}, u32[]{:S(2)}, u32[]{:S(2)}) %collective-permute-start.20) | collective-permute-done | bytes 262176 | tf_op jit(solution)/shard_map/ppermute | solution.py:486
  116.4 4.4 collective-permute-done.21
  124.4 16.1 %layer_forward.3 = (bf16[256,1024]{1,0:T(8,128)(2,1)}, bf16[256,2048]{1,0:T(8,128)(2,1)}, bf16[256,2304]{1,0:T(8,128)(2,1)}, f32[256,32]{1,0:T(8,128)}, f32[256,...) custom-call(bf16[256,1024]{1,0:T(8,128)(2,1)} %slice_bitcast_fusion.9.u_ref, ...), custom_call_target="tpu_custom_call" | custom-call | flops 3909091328 | bytes 13172736 | tf_op jit(solution)/shard_map/layer_forward/pallas_call | solution.py:218
  140.5 3.5 collective-permute-start.24
  144.0 11.8 %collective-permute-done.24 = bf16[256,1024]{1,0:T(8,128)(2,1)S(1)} collective-permute-done((bf16[256,1024]{1,0:T(8,128)(2,1)}, bf16[256,1024]{1,0:T(8,128)(2,1)S(1)}, u32[]{:S(2)}, u32[]{:S(2)}) %collective-permute-start.24) | collective-permute-done | bytes 524320 | tf_op jit(solution)/shard_map/ppermute | solution.py:618
  157.9 16.1 %layer_forward.4 = (bf16[256,1024]{1,0:T(8,128)(2,1)}, bf16[256,2048]{1,0:T(8,128)(2,1)}, bf16[256,2304]{1,0:T(8,128)(2,1)}, f32[256,32]{1,0:T(8,128)}, f32[256,...) custom-call(bf16[256,1024]{1,0:T(8,128)(2,1)} %bitcast_select_fusion.1.u_ref, ...), custom_call_target="tpu_custom_call" | custom-call | flops 3909091328 | bytes 13172736 | tf_op jit(solution)/shard_map/layer_forward/pallas_call | solution.py:218
  174.0 4.3 collective-permute-start.26
  180.9 25.1 %layer_backward.3 = (bf16[256,4384]{1,0:T(8,128)(2,1)}, f32[256,1024]{1,0:T(8,128)}, f32[1,1024]{1,0:T(1,128)}, f32[4,2304]{1,0:T(4,128)}, f32[1,2304]{1,0:T(1,1...) custom-call(bf16[256,1024]{1,0:T(8,128)(2,1)} %bitcast_select_fusion.1.u_ref, ...), custom_call_target="tpu_custom_call" | custom-call | flops 4445962240 | bytes 22151168 | tf_op jit(solution)/shard_map/layer_backward/pallas_call | solution.py:436
  210.9 16.0 %layer_forward.5 = (bf16[256,1024]{1,0:T(8,128)(2,1)}, bf16[256,2048]{1,0:T(8,128)(2,1)}, bf16[256,2304]{1,0:T(8,128)(2,1)}, f32[256,32]{1,0:T(8,128)}, f32[256,...) custom-call(bf16[256,1024]{1,0:T(8,128)(2,1)} %broadcast_select_fusion.2.u_ref, ...), custom_call_target="tpu_custom_call" | custom-call | flops 3909091328 | bytes 13172736 | tf_op jit(solution)/shard_map/layer_forward/pallas_call | solution.py:218
  227.8 25.2 %layer_backward.4 = (bf16[256,4384]{1,0:T(8,128)(2,1)}, f32[256,1024]{1,0:T(8,128)}, f32[1,1024]{1,0:T(1,128)}, f32[4,2304]{1,0:T(4,128)}, f32[1,2304]{1,0:T(1,1...) custom-call(bf16[256,1024]{1,0:T(8,128)(2,1)} %broadcast_select_fusion.2.u_ref, ...), custom_call_target="tpu_custom_call" | custom-call | flops 4445962240 | bytes 22151168 | tf_op jit(solution)/shard_map/layer_backward/pallas_call | solution.py:436
  271.1 25.1 %layer_backward.5 = (bf16[256,4384]{1,0:T(8,128)(2,1)}, f32[256,1024]{1,0:T(8,128)}, f32[1,1024]{1,0:T(1,128)}, f32[4,2304]{1,0:T(4,128)}, f32[1,2304]{1,0:T(1,1...) custom-call(bf16[256,1024]{1,0:T(8,128)(2,1)} %bitcast_select_fusion.1.u_ref, ...), custom_call_target="tpu_custom_call" | custom-call | flops 4445962240 | bytes 22151168 | tf_op jit(solution)/shard_map/layer_backward/pallas_call | solution.py:436
  298.5 3.4 collective-permute-start.29
  303.8 4.0 fusion
  311.1 4.4 copy.43
  315.5 5.8 %fusion.1 = f32[256,4384]{0,1:T(8,128)} fusion(bf16[256,512]{1,0:T(8,128)(2,1)S(1)} %bitcast.298, bf16[256,4384]{1,0:T(8,128)(2,1)S(1)} %broadcast_select_fusion, bf16[256,4384]{1,0:T(8,128)(2,1)} %get-tuple-element.92), kind=kOutput, calls=%fused_computation.5 | convolution fusion | flops 1160462336 | bytes 9240576 | tf_op jit(solution)/shard_map/dot_general | solution.py:531
  321.3 3.3 convolution_convert_fusion.2
  324.6 4.3 copy.41
  337.6 5.9 %copy.42 = f32[256,4384]{1,0:T(8,128)} copy(f32[256,4384]{0,1:T(8,128)} %fusion) | data formatting | bytes 8978432 | tf_op jit(solution)/shard_map/convert_element_type | solution.py:545
  343.5 6.0 %copy.40 = f32[256,4384]{1,0:T(8,128)} copy(f32[256,4384]{0,1:T(8,128)} %fusion.1) | data formatting | bytes 8978432 | tf_op jit(solution)/shard_map/convert_element_type | solution.py:545
  357.7 10.3 %collective-permute-done.44 = bf16[128,1024]{1,0:T(8,128)(2,1)S(1)} collective-permute-done((bf16[128,1024]{1,0:T(8,128)(2,1)S(1)}, bf16[128,1024]{1,0:T(8,128)(2,1)S(1)}, u32[]{:S(2)}, u32[]{:S(2)}) %collective-permute-start.44) | collective-permute-done | bytes 262176 | tf_op jit(solution)/shard_map/ppermute | solution.py:481
  377.0 21.2 %collective-permute-done.32 = bf16[64,4384]{1,0:T(8,128)(2,1)S(1)} collective-permute-done((bf16[64,4384]{1,0:T(8,128)(2,1)S(1)}, bf16[64,4384]{1,0:T(8,128)(2,1)S(1)}, u32[]{:S(2)}, u32[]{:S(2)}) %collective-permute-start.32) | collective-permute-done | bytes 561184 | tf_op jit(solution)/shard_map/ppermute | solution.py:481
  403.2 12.9 %collective-permute-done.33 = bf16[64,4384]{1,0:T(8,128)(2,1)S(1)} collective-permute-done((bf16[64,4384]{1,0:T(8,128)(2,1)S(1)}, bf16[64,4384]{1,0:T(8,128)(2,1)S(1)}, u32[]{:S(2)}, u32[]{:S(2)}) %collective-permute-start.33) | collective-permute-done | bytes 561184 | tf_op jit(solution)/shard_map/ppermute | solution.py:486
  418.2 64.5 %psum.7 = f32[4,3672]{1,0:T(4,128)S(1)} all-reduce(f32[4,3672]{1,0:T(4,128)S(1)} %concatenate.43), channel_id=1, replica_groups=mesh['section'=2,'fsdp'=4,'dp'=4] {'fsdp','dp'}, use_global_device_ids=true, to_apply=%region_1.2 | all-reduce | flops 14688 | bytes 117504 | tf_op jit(solution)/shard_map/psum | solution.py:667
  492.9 3.7 collective-permute-done.49
  516.1 10.9 %collective-permute-done.39 = bf16[64,4384]{1,0:T(8,128)(2,1)S(1)} collective-permute-done((bf16[64,4384]{1,0:T(8,128)(2,1)S(1)}, bf16[64,4384]{1,0:T(8,128)(2,1)S(1)}, u32[]{:S(2)}, u32[]{:S(2)}) %collective-permute-start.39) | collective-permute-done | bytes 561184 | tf_op jit(solution)/shard_map/ppermute | solution.py:481
  530.3 5.9 %copy.60 = f32[1,256,4384]{1,2,0:T(8,128)} copy(f32[1,256,4384]{2,1,0:T(8,128)} %bitcast.82) | data formatting | bytes 8978432
  (349 shorter events, 143.8 us)
Async XLA Ops:
  4.7 36.1 %collective-permute-start = (bf16[64,4384]{1,0:T(8,128)(2,1)}, bf16[64,4384]{1,0:T(8,128)(2,1)}, u32[]{:S(2)}, u32[]{:S(2)}) collective-permute-start(bf16[64,4384]{1,0:T(8,128)(2,1)} %dynamic-slice_bitcast_fusion), channel_id=1, source_target_pairs={{0,4},{4,8},{8,12},{12,0},{1,5},{5,9},{9,13},{13,1},{2,6},{6,10},{... | collective-permute-start | bytes 1683464 | tf_op jit(solution)/shard_map/ppermute | solution.py:486
  40.8 19.4 %collective-permute-start.1 = (bf16[64,4384]{1,0:T(8,128)(2,1)}, bf16[64,4384]{1,0:T(8,128)(2,1)S(1)}, u32[]{:S(2)}, u32[]{:S(2)}) collective-permute-start(bf16[64,4384]{1,0:T(8,128)(2,1)} %collective-permute-done), channel_id=1, source_target_pairs={{0,2},{1,3},{2,0},{3,1},{4,6},{5,7},{6,4},{7,5},{8,10},{9,11},{10,... | collective-permute-start | bytes 1683464 | tf_op jit(solution)/shard_map/ppermute | solution.py:481
  42.3 19.3 %collective-permute-start.2 = (bf16[64,4384]{1,0:T(8,128)(2,1)}, bf16[64,4384]{1,0:T(8,128)(2,1)S(1)}, u32[]{:S(2)}, u32[]{:S(2)}) collective-permute-start(bf16[64,4384]{1,0:T(8,128)(2,1)} %collective-permute-done), channel_id=1, source_target_pairs={{0,1},{1,0},{2,3},{3,2},{4,5},{5,4},{6,7},{7,6},{8,9},{9,8},{10,11... | collective-permute-start | bytes 1683464 | tf_op jit(solution)/shard_map/ppermute | solution.py:481
  42.3 17.4 %collective-permute-start.4 = (bf16[64,4384]{1,0:T(8,128)(2,1)}, bf16[64,4384]{1,0:T(8,128)(2,1)S(1)}, u32[]{:S(2)}, u32[]{:S(2)}) collective-permute-start(bf16[64,4384]{1,0:T(8,128)(2,1)} %collective-permute-done), channel_id=1, source_target_pairs={{0,4},{4,8},{8,12},{12,0},{1,5},{5,9},{9,13},{13,1},{2,6},{6,10},{... | collective-permute-start | bytes 1683464 | tf_op jit(solution)/shard_map/ppermute | solution.py:486
  59.7 19.2 %collective-permute-start.5 = (bf16[64,4384]{1,0:T(8,128)(2,1)S(1)}, bf16[64,4384]{1,0:T(8,128)(2,1)S(1)}, u32[]{:S(2)}, u32[]{:S(2)}) collective-permute-start(bf16[64,4384]{1,0:T(8,128)(2,1)S(1)} %collective-permute-done.4), channel_id=1, source_target_pairs={{0,2},{1,3},{2,0},{3,1},{4,6},{5,7},{6,4},{7,5},{8,10},{9,11},{10,... | collective-permute-start | bytes 1683464 | tf_op jit(solution)/shard_map/ppermute | solution.py:481
  60.2 28.4 %collective-permute-start.6 = (bf16[64,4384]{1,0:T(8,128)(2,1)S(1)}, bf16[64,4384]{1,0:T(8,128)(2,1)S(1)}, u32[]{:S(2)}, u32[]{:S(2)}) collective-permute-start(bf16[64,4384]{1,0:T(8,128)(2,1)S(1)} %collective-permute-done.4), channel_id=1, source_target_pairs={{0,1},{1,0},{2,3},{3,2},{4,5},{5,4},{6,7},{7,6},{8,9},{9,8},{10,11... | collective-permute-start | bytes 1683464 | tf_op jit(solution)/shard_map/ppermute | solution.py:481
  60.2 17.2 %collective-permute-start.8 = (bf16[64,4384]{1,0:T(8,128)(2,1)S(1)}, bf16[64,4384]{1,0:T(8,128)(2,1)S(1)}, u32[]{:S(2)}, u32[]{:S(2)}) collective-permute-start(bf16[64,4384]{1,0:T(8,128)(2,1)S(1)} %collective-permute-done.4), channel_id=1, source_target_pairs={{0,4},{4,8},{8,12},{12,0},{1,5},{5,9},{9,13},{13,1},{2,6},{6,10},{... | collective-permute-start | bytes 1683464 | tf_op jit(solution)/shard_map/ppermute | solution.py:486
  60.3 18.7 %collective-permute-start.3 = (bf16[64,4384]{1,0:T(8,128)(2,1)S(1)}, bf16[64,4384]{1,0:T(8,128)(2,1)S(1)}, u32[]{:S(2)}, u32[]{:S(2)}) collective-permute-start(bf16[64,4384]{1,0:T(8,128)(2,1)S(1)} %collective-permute-done.1), channel_id=1, source_target_pairs={{0,1},{1,0},{2,3},{3,2},{4,5},{5,4},{6,7},{7,6},{8,9},{9,8},{10,11... | collective-permute-start | bytes 1683464 | tf_op jit(solution)/shard_map/ppermute | solution.py:481
  77.4 25.0 %collective-permute-start.9 = (bf16[64,4384]{1,0:T(8,128)(2,1)S(1)}, bf16[64,4384]{1,0:T(8,128)(2,1)S(1)}, u32[]{:S(2)}, u32[]{:S(2)}) collective-permute-start(bf16[64,4384]{1,0:T(8,128)(2,1)S(1)} %collective-permute-done.8), channel_id=1, source_target_pairs={{0,2},{1,3},{2,0},{3,1},{4,6},{5,7},{6,4},{7,5},{8,10},{9,11},{10,... | collective-permute-start | bytes 1683464 | tf_op jit(solution)/shard_map/ppermute | solution.py:481
  78.9 21.7 %collective-permute-start.7 = (bf16[64,4384]{1,0:T(8,128)(2,1)S(1)}, bf16[64,4384]{1,0:T(8,128)(2,1)S(1)}, u32[]{:S(2)}, u32[]{:S(2)}) collective-permute-start(bf16[64,4384]{1,0:T(8,128)(2,1)S(1)} %collective-permute-done.5), channel_id=1, source_target_pairs={{0,1},{1,0},{2,3},{3,2},{4,5},{5,4},{6,7},{7,6},{8,9},{9,8},{10,11... | collective-permute-start | bytes 1683464 | tf_op jit(solution)/shard_map/ppermute | solution.py:481
  97.7 16.7 %collective-permute-start.15 = (bf16[128,1024]{1,0:T(8,128)(2,1)S(1)}, bf16[128,1024]{1,0:T(8,128)(2,1)S(1)}, u32[]{:S(2)}, u32[]{:S(2)}) collective-permute-start(bf16[128,1024]{1,0:T(8,128)(2,1)S(1)} %collective-permute-done.13), channel_id=1, source_target_pairs={{0,1},{1,0},{2,3},{3,2},{4,5},{5,4},{6,7},{7,6},{8,9},{9,8},{10,11... | collective-permute-start | bytes 786440 | tf_op jit(solution)/shard_map/ppermute | solution.py:481
  103.4 17.5 %collective-permute-start.11 = (bf16[64,4384]{1,0:T(8,128)(2,1)S(1)}, bf16[64,4384]{1,0:T(8,128)(2,1)S(1)}, u32[]{:S(2)}, u32[]{:S(2)}) collective-permute-start(bf16[64,4384]{1,0:T(8,128)(2,1)S(1)} %collective-permute-done.9), channel_id=1, source_target_pairs={{0,1},{1,0},{2,3},{3,2},{4,5},{5,4},{6,7},{7,6},{8,9},{9,8},{10,11... | collective-permute-start | bytes 1683464 | tf_op jit(solution)/shard_map/ppermute | solution.py:481
  174.0 34.7 %collective-permute-start.26 = (bf16[256,1024]{1,0:T(8,128)(2,1)}, bf16[256,1024]{1,0:T(8,128)(2,1)S(1)}, u32[]{:S(2)}, u32[]{:S(2)}) collective-permute-start(bf16[256,1024]{1,0:T(8,128)(2,1)} %get-tuple-element.56), channel_id=1, source_target_pairs={{0,16},{1,17},{2,18},{3,19},{4,20},{5,21},{6,22},{7,23},{8,24},{9,... | collective-permute-start | bytes 1572872 | tf_op jit(solution)/shard_map/ppermute | solution.py:618
  179.2 87.4 %collective-permute-start.25 = (bf16[256,1024]{1,0:T(8,128)(2,1)}, bf16[256,1024]{1,0:T(8,128)(2,1)}, u32[]{:S(2)}, u32[]{:S(2)}) collective-permute-start(bf16[256,1024]{1,0:T(8,128)(2,1)} %get-tuple-element.56), channel_id=1, source_target_pairs={{16,0},{17,1},{18,2},{19,3},{20,4},{21,5},{22,6},{23,7},{24,8},{25... | collective-permute-start | bytes 1572872 | tf_op jit(solution)/shard_map/ppermute | solution.py:621
  207.4 19.6 %collective-permute-start.27 = (bf16[256,1024]{1,0:T(8,128)(2,1)S(1)}, bf16[256,1024]{1,0:T(8,128)(2,1)S(1)}, u32[]{:S(2)}, u32[]{:S(2)}) collective-permute-start(bf16[256,1024]{1,0:T(8,128)(2,1)S(1)} %convert_element_type.218), channel_id=1, source_target_pairs={{16,0},{17,1},{18,2},{19,3},{20,4},{21,5},{22,6},{23,7},{24,8},{25... | collective-permute-start | bytes 1572872 | tf_op jit(solution)/shard_map/ppermute | solution.py:621
  255.2 15.9 %collective-permute-start.28 = (bf16[256,1024]{1,0:T(8,128)(2,1)}, bf16[256,1024]{1,0:T(8,128)(2,1)}, u32[]{:S(2)}, u32[]{:S(2)}) collective-permute-start(bf16[256,1024]{1,0:T(8,128)(2,1)} %convert_element_type.219), channel_id=1, source_target_pairs={{16,0},{17,1},{18,2},{19,3},{20,4},{21,5},{22,6},{23,7},{24,8},{25... | collective-permute-start | bytes 1572872 | tf_op jit(solution)/shard_map/ppermute | solution.py:621
  298.5 203.6 %collective-permute-start.29 = (bf16[256,1024]{1,0:T(8,128)(2,1)}, bf16[256,1024]{1,0:T(8,128)(2,1)}, u32[]{:S(2)}, u32[]{:S(2)}) collective-permute-start(bf16[256,1024]{1,0:T(8,128)(2,1)} %convert_element_type.220), channel_id=1, source_target_pairs={{0,16},{1,17},{2,18},{3,19},{4,20},{5,21},{6,22},{7,23},{8,24},{9,... | collective-permute-start | bytes 1572872 | tf_op jit(solution)/shard_map/ppermute | solution.py:618
  315.5 52.7 %collective-permute-start.31 = (bf16[4,64,4384]{2,1,0:T(8,128)(2,1)}, bf16[4,64,4384]{2,1,0:T(8,128)(2,1)}, u32[]{:S(2)}, u32[]{:S(2)}) collective-permute-start(bf16[4,64,4384]{2,1,0:T(8,128)(2,1)} %bitcast.70), channel_id=1, source_target_pairs={{0,1},{1,0},{2,3},{3,2},{4,5},{5,4},{6,7},{7,6},{8,9},{9,8},{10,11... | collective-permute-start | bytes 6733832 | tf_op jit(solution)/shard_map/ppermute | solution.py:481
  328.9 44.4 %collective-permute-start.30 = (bf16[4,64,4384]{2,1,0:T(8,128)(2,1)}, bf16[4,64,4384]{2,1,0:T(8,128)(2,1)S(1)}, u32[]{:S(2)}, u32[]{:S(2)}) collective-permute-start(bf16[4,64,4384]{2,1,0:T(8,128)(2,1)} %bitcast.288), channel_id=1, source_target_pairs={{0,1},{1,0},{2,3},{3,2},{4,5},{5,4},{6,7},{7,6},{8,9},{9,8},{10,11... | collective-permute-start | bytes 6733832 | tf_op jit(solution)/shard_map/ppermute | solution.py:481
  335.4 16.1 %collective-permute-start.43 = (bf16[4,128,1024]{2,1,0:T(8,128)(2,1)}, bf16[4,128,1024]{2,1,0:T(8,128)(2,1)}, u32[]{:S(2)}, u32[]{:S(2)}) collective-permute-start(bf16[4,128,1024]{2,1,0:T(8,128)(2,1)} %bitcast.108), channel_id=1, source_target_pairs={{0,1},{1,0},{2,3},{3,2},{4,5},{5,4},{6,7},{7,6},{8,9},{9,8},{10,11... | collective-permute-start | bytes 3145736 | tf_op jit(solution)/shard_map/ppermute | solution.py:481
  337.2 18.5 %collective-permute-start.42 = (bf16[4,128,1024]{2,1,0:T(8,128)(2,1)}, bf16[4,128,1024]{2,1,0:T(8,128)(2,1)}, u32[]{:S(2)}, u32[]{:S(2)}) collective-permute-start(bf16[4,128,1024]{2,1,0:T(8,128)(2,1)} %bitcast.95), channel_id=1, source_target_pairs={{0,1},{1,0},{2,3},{3,2},{4,5},{5,4},{6,7},{7,6},{8,9},{9,8},{10,11... | collective-permute-start | bytes 3145736 | tf_op jit(solution)/shard_map/ppermute | solution.py:481
  354.1 44.5 %collective-permute-start.46 = (bf16[128,1024]{1,0:T(8,128)(2,1)S(1)}, bf16[128,1024]{1,0:T(8,128)(2,1)S(1)}, u32[]{:S(2)}, u32[]{:S(2)}) collective-permute-start(bf16[128,1024]{1,0:T(8,128)(2,1)S(1)} %get-tuple-element.135), channel_id=1, source_target_pairs={{0,2},{1,3},{2,0},{3,1},{4,6},{5,7},{6,4},{7,5},{8,10},{9,11},{10,... | collective-permute-start | bytes 786440 | tf_op jit(solution)/shard_map/ppermute | solution.py:481
  368.1 32.1 %collective-permute-start.45 = (bf16[128,1024]{1,0:T(8,128)(2,1)S(1)}, bf16[128,1024]{1,0:T(8,128)(2,1)S(1)}, u32[]{:S(2)}, u32[]{:S(2)}) collective-permute-start(bf16[128,1024]{1,0:T(8,128)(2,1)S(1)} %fusion.17), channel_id=1, source_target_pairs={{0,4},{4,8},{8,12},{12,0},{1,5},{5,9},{9,13},{13,1},{2,6},{6,10},{... | collective-permute-start | bytes 786440 | tf_op jit(solution)/shard_map/ppermute | solution.py:486
  371.7 30.0 %collective-permute-start.34 = (bf16[64,4384]{1,0:T(8,128)(2,1)S(1)}, bf16[64,4384]{1,0:T(8,128)(2,1)S(1)}, u32[]{:S(2)}, u32[]{:S(2)}) collective-permute-start(bf16[64,4384]{1,0:T(8,128)(2,1)S(1)} %get-tuple-element.115), channel_id=1, source_target_pairs={{0,2},{1,3},{2,0},{3,1},{4,6},{5,7},{6,4},{7,5},{8,10},{9,11},{10,... | collective-permute-start | bytes 1683464 | tf_op jit(solution)/shard_map/ppermute | solution.py:481
  373.3 24.9 %collective-permute-start.32 = (bf16[64,4384]{1,0:T(8,128)(2,1)S(1)}, bf16[64,4384]{1,0:T(8,128)(2,1)S(1)}, u32[]{:S(2)}, u32[]{:S(2)}) collective-permute-start(bf16[64,4384]{1,0:T(8,128)(2,1)S(1)} %get-tuple-element.112), channel_id=1, source_target_pairs={{0,2},{1,3},{2,0},{3,1},{4,6},{5,7},{6,4},{7,5},{8,10},{9,11},{10,... | collective-permute-start | bytes 1683464 | tf_op jit(solution)/shard_map/ppermute | solution.py:481
  398.3 17.8 %collective-permute-start.33 = (bf16[64,4384]{1,0:T(8,128)(2,1)S(1)}, bf16[64,4384]{1,0:T(8,128)(2,1)S(1)}, u32[]{:S(2)}, u32[]{:S(2)}) collective-permute-start(bf16[64,4384]{1,0:T(8,128)(2,1)S(1)} %fusion.10), channel_id=1, source_target_pairs={{0,4},{4,8},{8,12},{12,0},{1,5},{5,9},{9,13},{13,1},{2,6},{6,10},{... | collective-permute-start | bytes 1683464 | tf_op jit(solution)/shard_map/ppermute | solution.py:486
  398.6 84.7 %collective-permute-start.48 = (bf16[128,1024]{1,0:T(8,128)(2,1)}, bf16[128,1024]{1,0:T(8,128)(2,1)}, u32[]{:S(2)}, u32[]{:S(2)}) collective-permute-start(bf16[128,1024]{1,0:T(8,128)(2,1)} %get-tuple-element.134), channel_id=1, source_target_pairs={{0,2},{1,3},{2,0},{3,1},{4,6},{5,7},{6,4},{7,5},{8,10},{9,11},{10,... | collective-permute-start | bytes 786440 | tf_op jit(solution)/shard_map/ppermute | solution.py:481
  401.0 82.3 %collective-permute-start.47 = (bf16[128,1024]{1,0:T(8,128)(2,1)}, bf16[128,1024]{1,0:T(8,128)(2,1)}, u32[]{:S(2)}, u32[]{:S(2)}) collective-permute-start(bf16[128,1024]{1,0:T(8,128)(2,1)} %fusion.16), channel_id=1, source_target_pairs={{0,4},{4,8},{8,12},{12,0},{1,5},{5,9},{9,13},{13,1},{2,6},{6,10},{... | collective-permute-start | bytes 786440 | tf_op jit(solution)/shard_map/ppermute | solution.py:486
  401.7 83.5 %collective-permute-start.36 = (bf16[64,4384]{1,0:T(8,128)(2,1)}, bf16[64,4384]{1,0:T(8,128)(2,1)}, u32[]{:S(2)}, u32[]{:S(2)}) collective-permute-start(bf16[64,4384]{1,0:T(8,128)(2,1)} %get-tuple-element.114), channel_id=1, source_target_pairs={{0,2},{1,3},{2,0},{3,1},{4,6},{5,7},{6,4},{7,5},{8,10},{9,11},{10,... | collective-permute-start | bytes 1683464 | tf_op jit(solution)/shard_map/ppermute | solution.py:481
  417.1 70.1 %collective-permute-start.35 = (bf16[64,4384]{1,0:T(8,128)(2,1)}, bf16[64,4384]{1,0:T(8,128)(2,1)}, u32[]{:S(2)}, u32[]{:S(2)}) collective-permute-start(bf16[64,4384]{1,0:T(8,128)(2,1)} %fusion.9), channel_id=1, source_target_pairs={{0,4},{4,8},{8,12},{12,0},{1,5},{5,9},{9,13},{13,1},{2,6},{6,10},{... | collective-permute-start | bytes 1683464 | tf_op jit(solution)/shard_map/ppermute | solution.py:486
  485.2 21.3 %collective-permute-start.38 = (bf16[64,4384]{1,0:T(8,128)(2,1)}, bf16[64,4384]{1,0:T(8,128)(2,1)}, u32[]{:S(2)}, u32[]{:S(2)}) collective-permute-start(bf16[64,4384]{1,0:T(8,128)(2,1)} %get-tuple-element.113), channel_id=1, source_target_pairs={{0,2},{1,3},{2,0},{3,1},{4,6},{5,7},{6,4},{7,5},{8,10},{9,11},{10,... | collective-permute-start | bytes 1683464 | tf_op jit(solution)/shard_map/ppermute | solution.py:481
  489.4 17.0 %collective-permute-start.37 = (bf16[64,4384]{1,0:T(8,128)(2,1)}, bf16[64,4384]{1,0:T(8,128)(2,1)}, u32[]{:S(2)}, u32[]{:S(2)}) collective-permute-start(bf16[64,4384]{1,0:T(8,128)(2,1)} %fusion.7), channel_id=1, source_target_pairs={{0,4},{4,8},{8,12},{12,0},{1,5},{5,9},{9,13},{13,1},{2,6},{6,10},{... | collective-permute-start | bytes 1683464 | tf_op jit(solution)/shard_map/ppermute | solution.py:486
  (80 other events, 1055.2 us)
